TPU v7x, 512 devices: a whole 4x8x8 slice. The times are simulated.
512 devices in a mesh: ep: 32 (over x_lo, z, core), et: 16 (over x_hi, y).
Axes of the slice: x: 4 (x_hi: 2, x_lo: 2; x = x_hi * 2 + x_lo), y: 8, z: 8, core: 2. Of those that a mesh axis runs over, the one named last changes fastest.
Arguments:
- tokens: bfloat16 [8192, 2048], P('ep', 'et'), may hold values from -6 to 6
- cotangent: bfloat16 [8192, 2048], P('ep', 'et'), may hold values from -1.5 to 1.5
- w_up: bfloat16 [32, 2048, 4096], P('ep', None, 'et'), may hold values from -0.1875 to 0.1875
- w_down: bfloat16 [32, 4096, 2048], P('ep', 'et'), may hold values from -0.09375 to 0.09375
- saved_pre: bfloat16 [32, 512, 4096], P('ep', None, 'et'), may hold values from -6 to 6
- gates: float32 [32, 512], P('ep'), may hold values from 0.25 to 2
- picks: int32 [32, 32, 16], P('ep'), may hold values from 0 to 255, as said below
- counts: int32 [32, 32], P('ep'), may hold values from 4 to 16, as said below
Outputs:
- grad_tokens: bfloat16 [8192, 2048], P('ep', 'et')
- grad_up: bfloat16 [32, 2048, 4096], P('ep', None, 'et')
- grad_down: bfloat16 [32, 4096, 2048], P('ep', 'et')
- gate_grad: float32 [32, 512], P('ep')
Inputs may be any that keep to these rules, and one draw needn't show every extreme that they name: For each ep index s and expert e the entries picks[s, e, :] are distinct tokens among that index's 256; slots k >= counts[s, e] are padding and are ignored. `counts`: some expert takes 16 tokens from every ep index.
All inputs are finite; a program needn't handle non-finite values.
Results may differ from a plain program's by a relative error of at most 0.0049.
Values may be sent and summed in bfloat16 or wider, within the bound.
No kernel may reach another device: no remote copies, remote signals or barrier semaphores. Data moves between devices by JAX's collectives and lax.ppermute only.
A program may use at most 64 MiB of HBM per device.

v0:
```python
import jax
import jax.numpy as jnp
from jax import lax
from jax.sharding import PartitionSpec as P


def per_device(tokens, cotangent, w_up, w_down, saved_pre, gates, picks, counts):
    local_idx = picks[0]
    n_experts, n_slots = local_idx.shape
    n_tokens = tokens.shape[0]
    slot_kept = lax.broadcasted_iota(jnp.int32, (n_experts, n_slots), 1) < counts[0][:, None]
    flat_idx = local_idx.reshape(-1)
    bf_zero = jnp.zeros((), tokens.dtype)
    picked_x = jnp.take(tokens, flat_idx, axis=0).reshape(n_experts, n_slots, -1)
    picked_y = jnp.take(cotangent, flat_idx, axis=0).reshape(n_experts, n_slots, -1)
    picked_x = jnp.where(slot_kept[:, :, None], picked_x, bf_zero)
    picked_y = jnp.where(slot_kept[:, :, None], picked_y, bf_zero)
    arrived_x, arrived_y = (
        lax.all_to_all(picked_x, "ep", split_axis=0, concat_axis=0, tiled=True),
        lax.all_to_all(picked_y, "ep", split_axis=0, concat_axis=0, tiled=True),
    )
    capacity = arrived_x.shape[0] * arrived_x.shape[1]
    arrived_x = arrived_x.reshape(capacity, -1)
    arrived_y = arrived_y.reshape(capacity, -1)
    full_x, full_y = (
        lax.all_gather(arrived_x, "et", axis=1, tiled=True),
        lax.all_gather(arrived_y, "et", axis=1, tiled=True),
    )
    w_first = w_up[0]
    w_second = w_down[0]
    pre_act = saved_pre[0]
    gate_row = gates[0]
    back_grad = lax.dot_general(
        full_y, w_second, (((1,), (1,)), ((), ())), preferred_element_type=jnp.float32
    )
    hidden = jnp.maximum(pre_act, jnp.zeros((), pre_act.dtype))
    expert_out = jnp.dot(hidden, w_second, preferred_element_type=jnp.float32)
    gate_term = jnp.sum(expert_out * full_y.astype(jnp.float32), axis=1)
    gate_total = lax.psum(gate_term, "et")
    pre_grad = (gate_row[:, None] * back_grad * (pre_act > 0)).astype(jnp.bfloat16)
    out_grad = (gate_row[:, None] * full_y.astype(jnp.float32)).astype(jnp.bfloat16)
    down_grad = lax.dot_general(
        hidden, out_grad, (((0,), (0,)), ((), ())), preferred_element_type=jnp.float32
    )
    up_grad = lax.dot_general(
        full_x, pre_grad, (((0,), (0,)), ((), ())), preferred_element_type=jnp.float32
    )
    positions = lax.broadcasted_iota(jnp.int32, (n_experts * n_slots, n_tokens), 1)
    selector = ((flat_idx[:, None] == positions) & slot_kept.reshape(-1)[:, None]).astype(
        jnp.float32
    )
    summed = lax.psum_scatter(
        lax.dot_general(
            w_first, pre_grad, (((1,), (1,)), ((), ())), preferred_element_type=jnp.float32
        ),
        "et",
        scatter_dimension=0,
        tiled=True,
    )
    returned = lax.all_to_all(summed, "ep", split_axis=1, concat_axis=1, tiled=True)
    token_grad = lax.dot_general(
        selector,
        returned,
        (((0,), (1,)), ((), ())),
        precision=lax.Precision.HIGHEST,
        preferred_element_type=jnp.float32,
    )
    return (
        token_grad.astype(jnp.bfloat16),
        up_grad.astype(jnp.bfloat16)[None],
        down_grad.astype(jnp.bfloat16)[None],
        gate_total[None],
    )


def solution(mesh):
    in_specs = (
        P("ep", "et"),
        P("ep", "et"),
        P("ep", None, "et"),
        P("ep", "et", None),
        P("ep", None, "et"),
        P("ep", None),
        P("ep", None, None),
        P("ep", None),
    )
    out_specs = (P("ep", "et"), P("ep", None, "et"), P("ep", "et", None), P("ep", None))
    return jax.shard_map(
        per_device, mesh=mesh, in_specs=in_specs, out_specs=out_specs, check_vma=False
    )
```

profile of v0, /device:TPU:1, one launch (start us, length us, event | category | flops | bytes accessed | tf_op | source)
XLA Modules:
  0.0 442.3 jit_solution(6837022788889596169)
XLA Ops:
  7.2 0.0 copy-start
  7.2 0.0 copy-start.3
  7.2 0.0 copy-start.2
  7.2 0.0 copy-start.4
  7.2 0.0 all-gather.3.cloned.1.call-start
  7.3 0.9 copy.12
  8.2 0.1 eq.10
  8.3 0.7 iota_compare_fusion.1
  9.0 1.9 gather_fusion.1
  10.9 1.9 gather_fusion
  12.8 0.1 broadcast_select_fusion
  13.0 0.1 broadcast_select_fusion.2
  13.1 21.9 %all_to_all.22 = bf16[32,16,128]{2,1,0:T(8,128)(2,1)} all-to-all(bf16[32,16,128]{2,1,0:T(8,128)(2,1)S(1)} %get-tuple-element.6), channel_id=1, replica_groups=mesh['ep'=32,'et'=16] {'ep'}, dimensions={0} | all-to-all | bytes 262144 | tf_op jit(solution)/shard_map/all_to_all | solution.py:20
  35.0 0.0 all-gather.3.cloned.1.call-update
  35.0 0.0 reduce-scatter.2.cloned.1.call-start
  35.1 84.0 %all-gather.3.cloned.1.call-done = bf16[512,2048]{1,0:T(8,128)(2,1)} async-done(((bf16[512,128]{1,0:T(8,128)(2,1)}), bf16[512,2048]{1,0:T(8,128)(2,1)}) %all-gather.3.cloned.1.call-update) | async-done | bytes 2097168 | tf_op jit(solution)/shard_map/all_gather | solution.py:27
  119.1 0.0 copy-done.3
  119.1 0.0 copy-done.2
  119.1 0.0 copy-done.4
  119.1 2.3 fusion.7
  121.4 0.0 copy-done
  121.4 2.7 convolution_bitcast_fusion
  124.1 0.0 copy-start.1
  124.1 0.0 reduce-scatter.2.cloned.1.call-update
  124.2 0.0 all-gather.5.cloned.1.call-start
  124.2 20.3 %all_to_all.23 = bf16[32,16,128]{2,1,0:T(8,128)(2,1)} all-to-all(bf16[32,16,128]{2,1,0:T(8,128)(2,1)S(1)} %get-tuple-element.5), channel_id=1, replica_groups=mesh['ep'=32,'et'=16] {'ep'}, dimensions={0} | all-to-all | bytes 262144 | tf_op jit(solution)/shard_map/all_to_all | solution.py:19
  144.5 0.0 all-gather.5.cloned.1.call-update
  144.5 0.1 lt.30
  144.6 0.0 copy-done.1
  144.6 2.1 fusion.1
  146.8 34.4 %psum.7 = f32[1,512]{1,0:T(1,128)} all-reduce(f32[1,512]{1,0:T(1,128)S(1)} %bitcast.41), channel_id=1, replica_groups=mesh['ep'=32,'et'=16] {'et'}, use_global_device_ids=true, to_apply=%region_2.4 | all-reduce | flops 512 | bytes 4096 | tf_op jit(solution)/shard_map/psum | solution.py:39
  181.2 156.2 %reduce-scatter.2.cloned.1.call-done = f32[128,512]{0,1:T(8,128)} async-done(((f32[2048,512]{0,1:T(8,128)}), f32[128,512]{0,1:T(8,128)}) %reduce-scatter.2.cloned.1.call-update) | async-done | bytes 262160 | tf_op jit(solution)/shard_map/reduce_scatter | solution.py:52
  337.4 12.8 %all-to-all-start.1 = ((f32[128,32,16]{0,2,1:T(8,128)}), f32[128,32,16]{0,2,1:T(8,128)S(1)}, u32[]{:S(2)}, u32[]{:S(2)}) async-start(f32[128,32,16]{0,2,1:T(8,128)} %bitcast.39), calls=%async_computation.2 | async-start | bytes 524288 | tf_op jit(solution)/shard_map/all_to_all | solution.py:60
  350.2 3.5 fusion.3
  353.7 77.3 %all-gather.5.cloned.1.call-done = bf16[512,2048]{1,0:T(8,128)(2,1)} async-done(((bf16[512,128]{1,0:T(8,128)(2,1)}), bf16[512,2048]{1,0:T(8,128)(2,1)}) %all-gather.5.cloned.1.call-update) | async-done | bytes 2097168 | tf_op jit(solution)/shard_map/all_gather | solution.py:26
  431.0 3.3 fusion.2
  434.4 0.0 all-to-all-done.1
  434.4 1.4 convolution_convert_fusion.2
  (3 shorter events, 0.0 us)
Async XLA Ops:
  7.2 114.3 %copy-start = (bf16[1,2048,256]{2,1,0:T(8,128)(2,1)S(1)}, bf16[1,2048,256]{2,1,0:T(8,128)(2,1)}, u32[]{:S(2)}) copy-start(bf16[1,2048,256]{2,1,0:T(8,128)(2,1)} %param.12) | copy-start | bytes 3145732
  7.2 111.9 %copy-start.3 = (bf16[1,512,256]{2,1,0:T(8,128)(2,1)S(1)}, bf16[1,512,256]{2,1,0:T(8,128)(2,1)}, u32[]{:S(2)}) copy-start(bf16[1,512,256]{2,1,0:T(8,128)(2,1)} %param.14) | copy-start | bytes 786436
  7.2 111.9 %copy-start.2 = (bf16[1,256,2048]{2,1,0:T(8,128)(2,1)S(1)}, bf16[1,256,2048]{2,1,0:T(8,128)(2,1)}, u32[]{:S(2)}) copy-start(bf16[1,256,2048]{2,1,0:T(8,128)(2,1)} %param.13) | copy-start | bytes 3145732
  7.2 111.9 %copy-start.4 = (f32[1,512]{1,0:T(1,128)S(1)}, f32[1,512]{1,0:T(1,128)}, u32[]{:S(2)}) copy-start(f32[1,512]{1,0:T(1,128)} %param.15) | copy-start | bytes 6148
  7.2 111.9 %all-gather.3.cloned.1.call-start = ((), (), s32[]{:S(2)}) async-start(), calls=%async_computation.4 | async-start | bytes 2228224 | tf_op jit(solution)/shard_map/all_gather | solution.py:27
  35.0 302.4 %reduce-scatter.2.cloned.1.call-start = ((), (), s32[]{:S(2)}) async-start(), calls=%async_computation.5 | async-start | bytes 4456448 | tf_op jit(solution)/shard_map/reduce_scatter | solution.py:52
  124.1 20.5 %copy-start.1 = (bf16[512,2048]{1,0:T(8,128)(2,1)S(1)}, bf16[512,2048]{1,0:T(8,128)(2,1)}, u32[]{:S(2)}) copy-start(bf16[512,2048]{1,0:T(8,128)(2,1)} %all-gather.3.cloned.1.call-done) | copy-start | bytes 6291460
  124.2 306.9 %all-gather.5.cloned.1.call-start = ((), (), s32[]{:S(2)}) async-start(), calls=%async_computation.6 | async-start | bytes 2228224 | tf_op jit(solution)/shard_map/all_gather | solution.py:26
  337.4 96.9 %all-to-all-start.1 = ((f32[128,32,16]{0,2,1:T(8,128)}), f32[128,32,16]{0,2,1:T(8,128)S(1)}, u32[]{:S(2)}, u32[]{:S(2)}) async-start(f32[128,32,16]{0,2,1:T(8,128)} %bitcast.39), calls=%async_computation.2 | async-start | bytes 524288 | tf_op jit(solution)/shard_map/all_to_all | solution.py:60
Sparse Core Ops, SparseCore 0:
  35.2 83.8 all-gather.2
  124.3 213.1 reduce-scatter.1
  340.9 90.0 all-gather.4
where the time goes:
time: 445 us; the launch traced here: 442 us
  waiting for transfers between devices  318 us (71%)
  blocking collectives  76.6 us (17%)
  matrix products  15.4 us (3%)
  between operations  13.8 us (3%)
  starting transfers between devices  12.9 us (3%)
  local copies, waits for them, and re-layouts  4.93 us (1%)
    reduce_scatter x1, waiting for transfers between devices, per_device(): lax.psum_scatter(lax.dot_general(w_first, pre_grad, (((1,), (1,)), ((), (...  156 us
    all_gather x1, waiting for transfers between devices, per_device(): lax.all_gather(arrived_y, 'et', axis=1, tiled=True)  84 us
    all_gather x1, waiting for transfers between devices, per_device(): lax.all_gather(arrived_x, 'et', axis=1, tiled=True)  77.3 us
    psum x1, blocking collectives, per_device(): gate_total = lax.psum(gate_term, 'et')  34.4 us
    all_to_all x1, blocking collectives, per_device(): lax.all_to_all(picked_y, 'ep', split_axis=0, concat_axis=0, tiled=True)  21.9 us
    all_to_all x1, blocking collectives, per_device(): lax.all_to_all(picked_x, 'ep', split_axis=0, concat_axis=0, tiled=True)  20.3 us
    all_to_all x1, starting transfers between devices, per_device(): lax.all_to_all(summed, 'ep', split_axis=1, concat_axis=1, tiled=True)  12.8 us
  transfers between devices with their start and end apart: 4, of which 3 were waited for; matrix products, arithmetic and copies ran while one was open for 2% of the time, Pallas kernels for 0%

commit v1 on v0

v1 whole, which is shorter than its diff:
```python
import jax
import jax.numpy as jnp
from jax import lax
from jax.experimental import pallas as pl
from jax.experimental.pallas import tpu as pltpu
from jax.sharding import Mesh, PartitionSpec as P

HI = 2
CHUNKS = 4
EXTRA = 16
NN = (((1,), (0,)), ((), ()))
NT = (((1,), (1,)), ((), ()))
TN = (((0,), (0,)), ((), ()))
VMEM_LIMIT = 56 << 20


def dot32(a, b, dims=NN):
    return lax.dot_general(a, b, dims, preferred_element_type=jnp.float32)


def pick_kernel(picks_ref, counts_ref, tokens_ref, cotangent_ref, sel_ref, out_ref):
    n_slots, n_experts = picks_ref.shape
    n_tokens = tokens_ref.shape[0]
    slot = lax.broadcasted_iota(jnp.int32, (n_slots, n_experts), 0)
    wanted = jnp.where(slot < counts_ref[...], picks_ref[...], -1)
    positions = lax.broadcasted_iota(jnp.int32, (n_slots, n_tokens), 1)
    for e in range(n_experts):
        hit = wanted[:, e : e + 1] == positions
        sel_ref[e * n_slots : (e + 1) * n_slots, :] = hit.astype(jnp.float32).astype(
            jnp.bfloat16
        )
    both = jnp.concatenate([tokens_ref[...], cotangent_ref[...]], axis=1)
    picked = dot32(sel_ref[...], both).astype(jnp.bfloat16)
    for h in range(HI):
        out_ref[h] = picked


def expert_kernel(
    full_hbm,
    down_hbm,
    pre_hbm,
    gate_hbm,
    up_hbm,
    pre_grad_ref,
    parts_hbm,
    y,
    down,
    pre,
    gate,
    up,
    parts,
    y_sem,
    down_sem,
    up_sem,
    out_sem,
    pre_sem,
    gate_sem,
):
    n_rows, n_hi, capacity, _ = full_hbm.shape
    n_blocks, _, width = parts_hbm.shape
    units = pre.shape[1]
    per = n_blocks // CHUNKS
    span = per * width
    y_copies, down_copies, up_copies = [], [], []
    for c in range(CHUNKS):
        down_copies.append(
            pltpu.make_async_copy(
                down_hbm.at[:, pl.ds(c * span, span)],
                down.at[:, pl.ds(c * span, span)],
                down_sem.at[c],
            )
        )
        down_copies[-1].start()
        for b in range(c * per, (c + 1) * per):
            y_copies.append(
                pltpu.make_async_copy(
                    full_hbm.at[b % n_rows, b // n_rows, :, pl.ds(width, width)],
                    y.at[:, pl.ds(b * width, width)],
                    y_sem.at[b],
                )
            )
            y_copies[-1].start()
    pre_copy = pltpu.make_async_copy(pre_hbm, pre, pre_sem)
    gate_copy = pltpu.make_async_copy(gate_hbm, gate, gate_sem)
    pre_copy.start()
    gate_copy.start()
    for c in range(CHUNKS):
        up_copies.append(
            pltpu.make_async_copy(
                up_hbm.at[pl.ds(c * span, span)], up.at[pl.ds(c * span, span)], up_sem.at[c]
            )
        )
        up_copies[-1].start()
    back = jnp.zeros((capacity, units), jnp.float32)
    for c in range(CHUNKS):
        down_copies[c].wait()
        for b in range(c * per, (c + 1) * per):
            y_copies[b].wait()
        columns = slice(c * span, (c + 1) * span)
        back += dot32(y[:, columns], down[:, columns], NT)
    pre_copy.wait()
    gate_copy.wait()
    act = pre[...].astype(jnp.float32)
    pre_grad = jnp.where(act > 0, gate[...] * back, 0.0).astype(jnp.bfloat16)
    pre_grad_ref[...] = pre_grad
    row_sum = lax.dot_general(
        jnp.ones((8, units), jnp.float32),
        jnp.maximum(act, 0.0) * back,
        NT,
        precision=lax.Precision.HIGHEST,
        preferred_element_type=jnp.float32,
    )
    rows = lax.broadcasted_iota(jnp.int32, (8, width), 0)
    n_gate = capacity // width
    packed = jnp.zeros((8, width), jnp.float32)
    for k in range(n_gate):
        packed = jnp.where(
            rows % n_gate == k, row_sum[:, k * width : (k + 1) * width], packed
        )
    high = packed.astype(jnp.bfloat16).astype(jnp.float32)
    packed = jnp.where(rows < n_gate, high, packed - high)
    packed = jnp.concatenate([packed, jnp.zeros_like(packed)], axis=0).astype(
        jnp.bfloat16
    )
    out_copies = []
    for c in range(CHUNKS):
        up_copies[c].wait()
        part = dot32(pre_grad, up[c * span : (c + 1) * span, :], NT).astype(jnp.bfloat16)
        for b in range(per):
            parts[c * per + b, :capacity, :] = part[:, b * width : (b + 1) * width]
            parts[c * per + b, capacity:, :] = packed
        out_copies.append(
            pltpu.make_async_copy(
                parts.at[pl.ds(c * per, per)], parts_hbm.at[pl.ds(c * per, per)], out_sem.at[c]
            )
        )
        out_copies[-1].start()
    for copy in out_copies:
        copy.wait()


def down_kernel(y0_ref, y1_ref, pre_ref, gate_ref, out_ref, hidden_t):
    @pl.when(pl.program_id(0) == 0)
    def _():
        hidden_t[...] = (
            jnp.maximum(pre_ref[...].astype(jnp.float32), 0.0).T.astype(jnp.bfloat16)
        )

    pair = jnp.concatenate([y0_ref[0, 0], y1_ref[0, 0]], axis=1)
    scaled = (gate_ref[...] * pair.astype(jnp.float32)).astype(jnp.bfloat16)
    out_ref[...] = dot32(hidden_t[...], scaled).astype(jnp.bfloat16)


def up_kernel(x0_ref, x1_ref, pre_grad_ref, out_ref):
    pair = jnp.concatenate([x0_ref[0, 0], x1_ref[0, 0]], axis=1)
    out_ref[...] = dot32(pair, pre_grad_ref[...], TN).astype(jnp.bfloat16)


def combine_kernel(sel_ref, returned_ref, out_ref):
    out_ref[...] = dot32(sel_ref[...], returned_ref[...], TN).astype(jnp.bfloat16)


def cost(flops, nbytes):
    return pl.CostEstimate(flops=flops, bytes_accessed=nbytes, transcendentals=0)


def per_device(tokens, cotangent, w_up, w_down, saved_pre, gates, picks, counts):
    bf16 = jnp.bfloat16
    n_tokens, width = tokens.shape
    _, n_experts, n_slots = picks.shape
    _, d_model, units = w_up.shape
    capacity = n_experts * n_slots
    n_blocks = d_model // width
    n_rows = n_blocks // HI
    n_pairs = n_blocks // 2
    macs = capacity * units * d_model
    params = pltpu.CompilerParams(vmem_limit_bytes=VMEM_LIMIT)
    shape = jax.ShapeDtypeStruct
    whole = lambda *dims: pl.BlockSpec(dims, lambda i, *_: (0,) * len(dims))
    hbm = pl.BlockSpec(memory_space=pl.ANY)
    vmem = pl.BlockSpec(memory_space=pltpu.VMEM)

    selector, picked = pl.pallas_call(
        pick_kernel,
        out_shape=(
            shape((capacity, n_tokens), bf16),
            shape((HI, capacity, 2 * width), bf16),
        ),
    )(picks[0].T, counts, tokens, cotangent)
    arrived = lax.all_to_all(
        picked.reshape(HI * n_experts, n_slots, 2 * width), ("hi", "ep"), 0, 0, tiled=True
    ).reshape(HI, capacity, 2 * width)
    full = lax.all_gather(arrived, "row", axis=0, tiled=False)

    gate_column = gates[0][:, None]
    pre_grad, parts = pl.pallas_call(
        expert_kernel,
        in_specs=[hbm] * 5,
        out_specs=[vmem, hbm],
        out_shape=(
            shape((capacity, units), bf16),
            shape((n_blocks, capacity + EXTRA, width), bf16),
        ),
        scratch_shapes=[
            pltpu.VMEM((capacity, d_model), bf16),
            pltpu.VMEM((units, d_model), bf16),
            pltpu.VMEM((capacity, units), bf16),
            pltpu.VMEM((capacity, 1), jnp.float32),
            pltpu.VMEM((d_model, units), bf16),
            pltpu.VMEM((n_blocks, capacity + EXTRA, width), bf16),
            pltpu.SemaphoreType.DMA((n_blocks,)),
            pltpu.SemaphoreType.DMA((CHUNKS,)),
            pltpu.SemaphoreType.DMA((CHUNKS,)),
            pltpu.SemaphoreType.DMA((CHUNKS,)),
            pltpu.SemaphoreType.DMA,
            pltpu.SemaphoreType.DMA,
        ],
        compiler_params=params,
        cost_estimate=cost(4 * macs, 7 << 20),
    )(full, w_down[0], saved_pre[0], gate_column, w_up[0])
    swapped = lax.all_to_all(parts, ("hi", "row"), 0, 0, tiled=True)

    def block(which, odd):
        def place(i):
            first = 2 * i + odd
            return first % n_rows, first // n_rows, 0, which
        return pl.BlockSpec((1, 1, capacity, width), place)

    grad_down = pl.pallas_call(
        down_kernel,
        grid=(n_pairs,),
        in_specs=[block(1, 0), block(1, 1), whole(capacity, units), whole(capacity, 1)],
        out_specs=pl.BlockSpec((units, 2 * width), lambda i: (0, i)),
        out_shape=shape((units, d_model), bf16),
        scratch_shapes=[pltpu.VMEM((units, capacity), bf16)],
        compiler_params=params,
        cost_estimate=cost(2 * macs, 4 << 20),
    )(full, full, saved_pre[0], gate_column)
    grad_up = pl.pallas_call(
        up_kernel,
        grid=(n_pairs,),
        in_specs=[block(0, 0), block(0, 1), whole(capacity, units)],
        out_specs=pl.BlockSpec((2 * width, units), lambda i: (i, 0)),
        out_shape=shape((d_model, units), bf16),
        compiler_params=params,
        cost_estimate=cost(2 * macs, 4 << 20),
    )(full, full, pre_grad)

    swapped, grad_down, grad_up = lax.optimization_barrier((swapped, grad_down, grad_up))
    summed = jnp.sum(swapped[:, :capacity].astype(jnp.float32), axis=0).astype(bf16)
    n_gate = capacity // width
    gate_rows = jnp.sum(swapped[:, capacity:].astype(jnp.float32), axis=0)
    gate_total = (gate_rows[:n_gate] + gate_rows[n_gate : 2 * n_gate]).reshape(1, capacity)
    returned = lax.all_to_all(
        summed.reshape(n_experts, n_slots, width), "ep", 0, 0, tiled=True
    ).reshape(capacity, width)
    grad_tokens = pl.pallas_call(
        combine_kernel, out_shape=shape((n_tokens, width), bf16)
    )(selector, returned)
    return grad_tokens, grad_up[None], grad_down[None], gate_total


def solution(mesh):
    n_ep, n_et = mesh.devices.shape
    fine = Mesh(mesh.devices.reshape(n_ep, HI, n_et // HI), ("ep", "hi", "row"))
    et = ("hi", "row")
    in_specs = (
        P("ep", et),
        P("ep", et),
        P("ep", None, et),
        P("ep", et, None),
        P("ep", None, et),
        P("ep", None),
        P("ep", None, None),
        P("ep", None),
    )
    out_specs = (P("ep", et), P("ep", None, et), P("ep", et, None), P("ep", None))
    return jax.shard_map(
        per_device, mesh=fine, in_specs=in_specs, out_specs=out_specs, check_vma=False
    )
```

time: 445 us -> 191 us (0.43)
  waiting for transfers between devices: 318 us -> 98.1 us
  blocking collectives: 76.6 us -> 32.3 us
  Pallas kernels: 0 us -> 24.9 us
  matrix products: 15.4 us -> 0 us
    reduce_scatter x1 -> x0, waiting for transfers between devices: 156 us -> none  [per_device(): lax.psum_scatter(lax.dot_general(w_first, pre_grad, (((1,), (1,)), ((), (...]
    all_gather x2 -> x1, waiting for transfers between devices: 161 us -> 52.7 us  [per_device(): full = lax.all_gather(arrived, 'row', axis=0, tiled=False)]
    all_to_all x1 -> x2, waiting for transfers between devices: 0.01 us -> 45.4 us  [the longest x1 36.9 us: per_device(): swapped = lax.all_to_all(parts, ('hi', 'row'), 0, 0, tiled=True)]
    psum x1 -> x0, blocking collectives: 34.4 us -> none  [per_device(): gate_total = lax.psum(gate_term, 'et')]
    pallas_call x0 -> x5, Pallas kernels: none -> 24.9 us  [the longest x1 7.29 us: per_device(): pl.pallas_call(expert_kernel, in_specs=[hbm] * 5, out_specs=[vmem, hbm],...]
    dot_general x6 -> x0, matrix products: 15.4 us -> none  [the longest x1 3.48 us: per_device(): lax.dot_general(hidden, out_grad, (((0,), (0,)), ((), ())), preferred_ele...]
    all_to_all x2 -> x1, blocking collectives: 42.2 us -> 32.3 us  [per_device(): lax.all_to_all(picked.reshape(HI * n_experts, n_slots, 2 * width), ('hi',...]
    all_to_all x1 -> x2, starting transfers between devices: 12.8 us -> 16.6 us  [the longest x1 9.87 us: per_device(): lax.all_to_all(summed.reshape(n_experts, n_slots, width), 'ep', 0, 0, til...]
  transfers between devices with their start and end apart: 4 -> 3, of which waited for: 3 -> 3; matrix products, arithmetic and copies ran while one was open for 2% -> 1% of each run, Pallas kernels for 0% -> 7%
where the time goes in v1:
time: 191 us; the launch traced here: 190 us
  waiting for transfers between devices  98.1 us (51%)
  blocking collectives  32.3 us (17%)
  Pallas kernels  24.9 us (13%)
  starting transfers between devices  16.6 us (9%)
  between operations  14.1 us (7%)
  local copies, waits for them, and re-layouts  2.19 us (1%)
    all_gather x1, waiting for transfers between devices, per_device(): full = lax.all_gather(arrived, 'row', axis=0, tiled=False)  52.7 us
    all_to_all x1, waiting for transfers between devices, per_device(): swapped = lax.all_to_all(parts, ('hi', 'row'), 0, 0, tiled=True)  36.9 us
    all_to_all x1, blocking collectives, per_device(): lax.all_to_all(picked.reshape(HI * n_experts, n_slots, 2 * width), ('hi',...  32.3 us
    all_to_all x1, starting transfers between devices, per_device(): lax.all_to_all(summed.reshape(n_experts, n_slots, width), 'ep', 0, 0, til...  9.87 us
    all_to_all x1, waiting for transfers between devices, per_device(): lax.all_to_all(summed.reshape(n_experts, n_slots, width), 'ep', 0, 0, til...  8.45 us
    pallas_call x1, Pallas kernels, per_device(): pl.pallas_call(expert_kernel, in_specs=[hbm] * 5, out_specs=[vmem, hbm],...  7.29 us
    pallas_call x1, Pallas kernels, per_device(): pl.pallas_call(down_kernel, grid=(n_pairs,), in_specs=[block(1, 0), block...  7.13 us
    all_to_all x1, starting transfers between devices, per_device(): swapped = lax.all_to_all(parts, ('hi', 'row'), 0, 0, tiled=True)  6.72 us
  transfers between devices with their start and end apart: 3, of which 3 were waited for; matrix products, arithmetic and copies ran while one was open for 1% of the time, Pallas kernels for 7%

profile of v1, /device:TPU:1, one launch (start us, length us, event | category | flops | bytes accessed | tf_op | source)
XLA Modules:
  0.0 189.7 jit_solution(17593736980598154177)
XLA Ops:
  7.2 0.0 all-gather.2.cloned.1.call-start
  7.2 2.0 %shard_map.111 = (bf16[512,256]{1,0:T(8,128)(2,1)}, bf16[2,512,256]{2,1,0:T(8,128)(2,1)}) custom-call(s32[16,32]{1,0:T(8,128)} %bitcast.23, s32[1,32]{1,0:T(1,128)} %counts_ref.1, bf16[256,128]{1,0:T(8,128)(2,1)} %tokens_ref.1, bf16[256,128]{1,0:T(8,128)(2,1)} %cotangent_ref.1), custom_call_target="tpu_custom_call" | custom-call | tf_op jit(solution)/shard_map/pallas_call | solution.py:183
  9.2 32.3 %all_to_all.15 = bf16[64,16,256]{2,1,0:T(8,128)(2,1)} all-to-all(bf16[64,16,256]{2,1,0:T(8,128)(2,1)} %bitcast.22), channel_id=1, replica_groups=mesh['ep'=32,'hi'=2,'row'=8] {'hi','ep'}, dimensions={0} | all-to-all | bytes 1048576 | tf_op jit(solution)/shard_map/all_to_all | solution.py:190
  41.5 0.0 all-gather.2.cloned.1.call-update
  41.5 1.5 copy.14.gate_hbm.gate_ref
  43.0 52.7 %all-gather.2.cloned.1.call-done.full_hbm.y0_ref.y1_ref.x0_ref.x1_ref = bf16[8,2,512,256]{3,2,1,0:T(8,128)(2,1)} async-done(((bf16[1,2,512,256]{3,2,1,0:T(8,128)(2,1)}), bf16[8,2,512,256]{3,2,1,0:T(8,128)(2,1)}) %all-gather.2.cloned.1.call-update) | async-done | bytes 4194320 | tf_op jit(solution)/shard_map/all_gather | solution.py:193
  95.7 7.3 %shard_map.112 = (bf16[512,256]{1,0:T(8,128)(2,1)}, bf16[16,528,128]{2,1,0:T(8,128)(2,1)}) custom-call(bf16[8,2,512,256]{3,2,1,0:T(8,128)(2,1)} %all-gather.2.cloned.1.call-done.full_hbm.y0_ref.y1_ref.x0_ref.x1_ref, bf16[256,2048]{1,0:T(8,128)(2,1)} %bitcast.17, bf16[512,256]{1,0:T(8,128)(2,1)} %bitcast.19, f32[512,1]{1,0:T(8,128)} %copy.14.gate_hbm.gate_ref, ...), custom_call_target="tpu_custom_call" | custom-call | flops 1073741824 | bytes 7340032 | tf_op jit(solution)/shard_map/pallas_call | solution.py:196
  103.0 6.7 %all-to-all-start.1 = ((bf16[16,528,128]{2,1,0:T(8,128)(2,1)}), bf16[16,528,128]{2,1,0:T(8,128)(2,1)S(1)}, u32[]{:S(2)}, u32[]{:S(2)}) async-start(bf16[16,528,128]{2,1,0:T(8,128)(2,1)} %get-tuple-element.13), calls=%async_computation.1 | async-start | bytes 4325376 | tf_op jit(solution)/shard_map/all_to_all | solution.py:221
  109.7 7.1 %shard_map.113 = bf16[256,2048]{1,0:T(8,128)(2,1)} custom-call(bf16[8,2,512,256]{3,2,1,0:T(8,128)(2,1)} %all-gather.2.cloned.1.call-done.full_hbm.y0_ref.y1_ref.x0_ref.x1_ref, bf16[8,2,512,256]{3,2,1,0:T(8,128)(2,1)} %all-gather.2.cloned.1.call-done.full_hbm.y0_ref.y1_ref.x0_ref.x1_ref, bf16[512,256]{1,0:T(8,128)(2,1)} %bitcast.20, ...), custom_call_target="tpu_custom_call" | custom-call | flops 536870912 | bytes 4194304 | tf_op jit(solution)/shard_map/pallas_call | solution.py:229
  116.9 6.6 %shard_map.114 = bf16[2048,256]{1,0:T(8,128)(2,1)} custom-call(bf16[8,2,512,256]{3,2,1,0:T(8,128)(2,1)} %all-gather.2.cloned.1.call-done.full_hbm.y0_ref.y1_ref.x0_ref.x1_ref, bf16[8,2,512,256]{3,2,1,0:T(8,128)(2,1)} %all-gather.2.cloned.1.call-done.full_hbm.y0_ref.y1_ref.x0_ref.x1_ref, bf16[512,256]{1,0:T(8,128)(2,1)} %get-tuple-element.14.pre_grad_ref), custom_call_target="tpu_custom_call" | custom-call | flops 536870912 | bytes 4194304 | tf_op jit(solution)/shard_map/pallas_call | solution.py:239
  123.5 36.9 %all-to-all-done.1 = bf16[16,528,128]{2,1,0:T(8,128)(2,1)S(1)} async-done(((bf16[16,528,128]{2,1,0:T(8,128)(2,1)}), bf16[16,528,128]{2,1,0:T(8,128)(2,1)S(1)}, u32[]{:S(2)}, u32[]{:S(2)}) %all-to-all-start.1) | async-done | bytes 2162720 | tf_op jit(solution)/shard_map/all_to_all | solution.py:221
  160.4 0.9 slice_reduce_fusion
  161.4 9.9 %all-to-all-start.2 = ((bf16[32,16,128]{2,1,0:T(8,128)(2,1)}), bf16[32,16,128]{2,1,0:T(8,128)(2,1)S(1)}, u32[]{:S(2)}, u32[]{:S(2)}) async-start(bf16[32,16,128]{2,1,0:T(8,128)(2,1)} %bitcast.8), calls=%async_computation.2 | async-start | bytes 262144 | tf_op jit(solution)/shard_map/all_to_all | solution.py:254
  171.3 0.6 slice_add_fusion
  171.8 8.5 %all-to-all-done.2 = bf16[32,16,128]{2,1,0:T(8,128)(2,1)S(1)} async-done(((bf16[32,16,128]{2,1,0:T(8,128)(2,1)}), bf16[32,16,128]{2,1,0:T(8,128)(2,1)S(1)}, u32[]{:S(2)}, u32[]{:S(2)}) %all-to-all-start.2) | async-done | bytes 131104 | tf_op jit(solution)/shard_map/all_to_all | solution.py:254
  180.3 0.0 copy-start
  180.3 0.7 copy-done
  180.9 1.9 shard_map.115
  (1 shorter events, 0.0 us)
Async XLA Ops:
  7.2 88.6 %all-gather.2.cloned.1.call-start = ((), (), s32[]{:S(2)}) async-start(), calls=%async_computation.3 | async-start | bytes 4718592 | tf_op jit(solution)/shard_map/all_gather | solution.py:193
  103.0 57.4 %all-to-all-start.1 = ((bf16[16,528,128]{2,1,0:T(8,128)(2,1)}), bf16[16,528,128]{2,1,0:T(8,128)(2,1)S(1)}, u32[]{:S(2)}, u32[]{:S(2)}) async-start(bf16[16,528,128]{2,1,0:T(8,128)(2,1)} %get-tuple-element.13), calls=%async_computation.1 | async-start | bytes 4325376 | tf_op jit(solution)/shard_map/all_to_all | solution.py:221
  161.4 18.9 %all-to-all-start.2 = ((bf16[32,16,128]{2,1,0:T(8,128)(2,1)}), bf16[32,16,128]{2,1,0:T(8,128)(2,1)S(1)}, u32[]{:S(2)}, u32[]{:S(2)}) async-start(bf16[32,16,128]{2,1,0:T(8,128)(2,1)} %bitcast.8), calls=%async_computation.2 | async-start | bytes 262144 | tf_op jit(solution)/shard_map/all_to_all | solution.py:254
  180.3 0.7 copy-start
Sparse Core Ops, SparseCore 0:
  41.6 54.0 all-gather.1

commit v2 on v1

v2 whole, which is shorter than its diff:
```python
import functools

import jax
import jax.numpy as jnp
from jax import lax
from jax.experimental import pallas as pl
from jax.experimental.pallas import tpu as pltpu
from jax.sharding import Mesh, PartitionSpec as P

HI = 2
EXTRA = 16
NN = (((1,), (0,)), ((), ()))
NT = (((1,), (1,)), ((), ()))
TN = (((0,), (0,)), ((), ()))
VMEM_LIMIT = 20 << 20


def dot32(a, b, dims=NN):
    return lax.dot_general(a, b, dims, preferred_element_type=jnp.float32)


def pick_kernel(picks_ref, counts_ref, tokens_ref, cotangent_ref, sel_ref, out_ref):
    n_slots, n_experts = picks_ref.shape
    n_tokens = tokens_ref.shape[0]
    slot = lax.broadcasted_iota(jnp.int32, (n_slots, n_experts), 0)
    wanted = jnp.where(slot < counts_ref[...], picks_ref[...], -1)
    positions = lax.broadcasted_iota(jnp.int32, (n_slots, n_tokens), 1)
    for e in range(n_experts):
        hit = wanted[:, e : e + 1] == positions
        sel_ref[e * n_slots : (e + 1) * n_slots, :] = hit.astype(jnp.float32).astype(
            jnp.bfloat16
        )
    both = jnp.concatenate([tokens_ref[...], cotangent_ref[...]], axis=1)
    picked = dot32(sel_ref[...], both).astype(jnp.bfloat16)
    for h in range(HI):
        out_ref[h] = picked


def place(order_ref, h, d):
    n_rows = order_ref.shape[0] // HI
    return pl.multiple_of(order_ref[h * n_rows + d % n_rows] * 128, 128)


def half_of(blocks, n, h, side):
    width = blocks[0].shape[-1] // 2
    if len(blocks) == 1:
        return blocks[0][h, :, side * width : (side + 1) * width]
    return blocks[h][0, :, side * width : (side + 1) * width]


def grouped(refs, distances, n_rows):
    groups, at = [], 0
    for d in distances:
        count = 2 if d == n_rows // 2 else 1
        groups.append(refs[at : at + count])
        at += count
    return groups, refs[at:]


def load_columns(order_ref, source, target, sems, distances, axis):
    copies = []
    for k, d in enumerate(distances):
        for h in range(HI):
            at = pl.ds(place(order_ref, h, d), 128)
            to = pl.ds((k * HI + h) * 128, 128)
            copies.append(
                pltpu.make_async_copy(
                    source.at[:, at] if axis else source.at[at],
                    target.at[:, to] if axis else target.at[to],
                    sems.at[k * HI + h],
                )
            )
            copies[-1].start()
    return copies


def back_kernel(distances, n_rows, last, order_ref, *refs):
    groups, rest = grouped(refs, distances, n_rows)
    if last:
        down_hbm, before_ref, pre_ref, gate_ref, pre_grad_ref, gate_out, down, sems = rest
    else:
        down_hbm, back_ref, down, sems = rest
    copies = load_columns(order_ref, down_hbm, down, sems, distances, 1)
    back = before_ref[...] if last else None
    for k in range(len(distances)):
        for h in range(HI):
            copies[k * HI + h].wait()
        pair = jnp.concatenate(
            [half_of(groups[k], n_rows, h, 1) for h in range(HI)], axis=1
        )
        term = dot32(pair, down[:, k * HI * 128 : (k + 1) * HI * 128], NT)
        back = term if back is None else back + term
    if not last:
        back_ref[...] = back
        return
    act = pre_ref[...].astype(jnp.float32)
    pre_grad_ref[...] = jnp.where(act > 0, gate_ref[...] * back, 0.0).astype(jnp.bfloat16)
    capacity, units = act.shape
    row_sum = lax.dot_general(
        jnp.ones((8, units), jnp.float32),
        jnp.maximum(act, 0.0) * back,
        NT,
        precision=lax.Precision.HIGHEST,
        preferred_element_type=jnp.float32,
    )
    rows = lax.broadcasted_iota(jnp.int32, (8, 128), 0)
    n_gate = capacity // 128
    packed = jnp.zeros((8, 128), jnp.float32)
    for k in range(n_gate):
        packed = jnp.where(
            rows % n_gate == k, row_sum[:, k * 128 : (k + 1) * 128], packed
        )
    high = packed.astype(jnp.bfloat16).astype(jnp.float32)
    packed = jnp.where(rows < n_gate, high, packed - high)
    gate_out[...] = jnp.concatenate([packed, jnp.zeros_like(packed)], axis=0)


def own_parts(order_ref, pre_grad_ref, up_hbm, up, sems, wanted):
    copies = []
    for k, (d, h) in enumerate(wanted):
        copies.append(
            pltpu.make_async_copy(
                up_hbm.at[pl.ds(place(order_ref, h, d), 128)],
                up.at[pl.ds(k * 128, 128)],
                sems.at[k],
            )
        )
        copies[-1].start()
    for copy in copies:
        copy.wait()
    parts = dot32(pre_grad_ref[...], up[...], NT)
    return [parts[:, k * 128 : (k + 1) * 128] for k in range(len(wanted))]


def first_kernel(d, h, order_ref, pre_grad_ref, gate_ref, up_hbm, out_ref, up, sems):
    (part,) = own_parts(order_ref, pre_grad_ref, up_hbm, up, sems, [(d, h)])
    capacity = pre_grad_ref.shape[0]
    out_ref[0, :capacity, :] = part.astype(jnp.bfloat16)
    out_ref[0, capacity:, :] = gate_ref[...].astype(jnp.bfloat16)


def pass_kernel(
    d, only, order_ref, came, pre_grad_ref, total_ref, up_hbm, out_ref, total_out, up, sems
):
    parts = own_parts(order_ref, pre_grad_ref, up_hbm, up, sems, [(d, 0), (d, 1)])
    capacity = pre_grad_ref.shape[0]
    for h in range(HI):
        part = parts[h]
        if only is None:
            part = part + came[h, :capacity, :].astype(jnp.float32)
        elif h == only:
            part = part + came[0, :capacity, :].astype(jnp.float32)
        out_ref[h, :capacity, :] = part.astype(jnp.bfloat16)
        out_ref[h, capacity:, :] = came[0, capacity:, :]
    total_out[...] = total_ref[...] + came[0, capacity:, :].astype(jnp.float32)


def last_kernel(
    order_ref, from_left, from_right, pre_grad_ref, total_left, total_right, up_hbm,
    sum_ref, gate_out, up, sems,
):
    parts = own_parts(order_ref, pre_grad_ref, up_hbm, up, sems, [(0, 0), (0, 1)])
    capacity = pre_grad_ref.shape[0]
    for h in range(HI):
        sum_ref[h] = (
            parts[h]
            + from_left[h, :capacity, :].astype(jnp.float32)
            + from_right[h, :capacity, :].astype(jnp.float32)
        ).astype(jnp.bfloat16)
    n_gate = capacity // 128
    total = total_left[...] + total_right[...] + from_left[0, capacity:, :].astype(jnp.float32)
    gate_out[...] = total[:n_gate] + total[n_gate : 2 * n_gate]


def down_kernel(distances, n_rows, more, order_ref, *refs):
    groups, rest = grouped(refs, distances, n_rows)
    if more:
        pre_ref, gate_ref, _, out_hbm, out, sems = rest
    else:
        pre_ref, gate_ref, out_hbm, out, sems = rest
    hidden_t = jnp.maximum(pre_ref[...].astype(jnp.float32), 0.0).T.astype(jnp.bfloat16)
    copies = []
    for k, d in enumerate(distances):
        pair = jnp.concatenate(
            [half_of(groups[k], n_rows, h, 1) for h in range(HI)], axis=1
        )
        scaled = (gate_ref[...] * pair.astype(jnp.float32)).astype(jnp.bfloat16)
        out[:, k * HI * 128 : (k + 1) * HI * 128] = dot32(hidden_t, scaled).astype(
            jnp.bfloat16
        )
        for h in range(HI):
            copies.append(
                pltpu.make_async_copy(
                    out.at[:, pl.ds((k * HI + h) * 128, 128)],
                    out_hbm.at[:, pl.ds(place(order_ref, h, d), 128)],
                    sems.at[k * HI + h],
                )
            )
            copies[-1].start()
    for copy in copies:
        copy.wait()


def up_kernel(distances, n_rows, more, order_ref, *refs):
    groups, rest = grouped(refs, distances, n_rows)
    if more:
        pre_grad_ref, _, out_hbm, out, sems = rest
    else:
        pre_grad_ref, out_hbm, out, sems = rest
    copies = []
    for k, d in enumerate(distances):
        pair = jnp.concatenate(
            [half_of(groups[k], n_rows, h, 0) for h in range(HI)], axis=1
        )
        out[k * HI * 128 : (k + 1) * HI * 128, :] = dot32(
            pair, pre_grad_ref[...], TN
        ).astype(jnp.bfloat16)
        for h in range(HI):
            copies.append(
                pltpu.make_async_copy(
                    out.at[pl.ds((k * HI + h) * 128, 128)],
                    out_hbm.at[pl.ds(place(order_ref, h, d), 128)],
                    sems.at[k * HI + h],
                )
            )
            copies[-1].start()
    for copy in copies:
        copy.wait()


def combine_kernel(sel_ref, returned_ref, out_ref):
    both = jnp.concatenate([returned_ref[h] for h in range(HI)], axis=1)
    total = dot32(sel_ref[...], both, TN)
    width = out_ref.shape[1]
    out_ref[...] = (total[:, :width] + total[:, width:]).astype(jnp.bfloat16)


def cost(flops, nbytes):
    return pl.CostEstimate(flops=flops, bytes_accessed=nbytes, transcendentals=0)


def per_device(tokens, cotangent, w_up, w_down, saved_pre, gates, picks, counts):
    bf16, f32 = jnp.bfloat16, jnp.float32
    n_tokens, width = tokens.shape
    _, n_experts, n_slots = picks.shape
    _, d_model, units = w_up.shape
    capacity = n_experts * n_slots
    n_rows = d_model // width // HI
    far = n_rows // 2
    macs = capacity * units * width * HI
    params = pltpu.CompilerParams(vmem_limit_bytes=VMEM_LIMIT)
    shape = jax.ShapeDtypeStruct
    hbm = pl.BlockSpec(memory_space=pl.ANY)
    vmem = pl.BlockSpec(memory_space=pltpu.VMEM)
    smem = pl.BlockSpec(memory_space=pltpu.SMEM)
    dma = pltpu.SemaphoreType.DMA

    def right(a):
        return lax.ppermute(a, "row", [(i, (i + 1) % n_rows) for i in range(n_rows)])

    def left(a):
        return lax.ppermute(a, "row", [(i, (i - 1) % n_rows) for i in range(n_rows)])

    hi, row = lax.axis_index("hi"), lax.axis_index("row")
    ahead_of = (row + jnp.arange(n_rows, dtype=jnp.int32)) % n_rows
    order = jnp.concatenate([h * n_rows + ahead_of for h in range(HI)])
    del hi
    gate_column = gates[0][:, None]
    pre, w_first, w_second = saved_pre[0], w_up[0], w_down[0]

    selector, picked = pl.pallas_call(
        pick_kernel,
        out_shape=(
            shape((capacity, n_tokens), bf16),
            shape((HI, capacity, 2 * width), bf16),
        ),
    )(picks[0].T, counts, tokens, cotangent)
    arrived = lax.all_to_all(
        picked.reshape(HI * n_experts, n_slots, 2 * width), ("hi", "ep"), 0, 0, tiled=True
    ).reshape(HI, capacity, 2 * width)

    blocks = {0: [arrived]}
    behind = ahead = arrived
    for d in range(1, far):
        behind, ahead = right(behind), left(ahead)
        blocks[-d], blocks[d] = [behind], [ahead]
    late = [far - 1, 1 - far, far]
    early = [d for d in blocks if d not in late]
    flat = lambda distances: [b for d in distances for b in blocks[d]]
    columns = lambda n: [pltpu.VMEM((units, n * HI * width), bf16), dma((n * HI,))]
    rows_of = lambda n: [pltpu.VMEM((n * width, units), bf16), dma((n,))]

    back = pl.pallas_call(
        functools.partial(back_kernel, early, n_rows, False),
        in_specs=[smem] + [vmem] * len(flat(early)) + [hbm],
        out_specs=vmem,
        out_shape=shape((capacity, units), f32),
        scratch_shapes=columns(len(early)),
        compiler_params=params,
        cost_estimate=cost(2 * macs * len(early), 4 << 20),
    )(order, *flat(early), w_second)
    down_early = pl.pallas_call(
        functools.partial(down_kernel, early, n_rows, False),
        in_specs=[smem] + [vmem] * (len(flat(early)) + 2),
        out_specs=hbm,
        out_shape=shape((units, d_model), bf16),
        scratch_shapes=columns(len(early)),
        compiler_params=params,
        cost_estimate=cost(2 * macs * len(early), 4 << 20),
    )(order, *flat(early), pre, gate_column)
    behind, ahead, back, down_early = lax.optimization_barrier(
        (behind, ahead, back, down_early)
    )
    blocks[1 - far], blocks[far - 1] = [behind], [ahead]
    blocks[far] = [right(behind[:1]), left(ahead[1:])]
    pre_grad, gate_mine = pl.pallas_call(
        functools.partial(back_kernel, late, n_rows, True),
        in_specs=[smem] + [vmem] * len(flat(late)) + [hbm, vmem, vmem, vmem],
        out_specs=[vmem, vmem],
        out_shape=(shape((capacity, units), bf16), shape((EXTRA, width), f32)),
        scratch_shapes=columns(len(late)),
        compiler_params=params,
        cost_estimate=cost(2 * macs * len(late), 3 << 20),
    )(order, *flat(late), w_second, back, pre, gate_column)

    grad_down = pl.pallas_call(
        functools.partial(down_kernel, late, n_rows, True),
        in_specs=[smem] + [vmem] * (len(flat(late)) + 2) + [hbm],
        out_specs=hbm,
        out_shape=shape((units, d_model), bf16),
        input_output_aliases={len(flat(late)) + 3: 0},
        scratch_shapes=columns(len(late)),
        compiler_params=params,
        cost_estimate=cost(2 * macs * len(late), 3 << 20),
    )(order, *flat(late), pre, gate_column, down_early)
    up_call = functools.partial(
        pl.pallas_call,
        out_specs=hbm,
        out_shape=shape((d_model, units), bf16),
        compiler_params=params,
        cost_estimate=cost(2 * macs * 4, 4 << 20),
    )
    up_early = up_call(
        functools.partial(up_kernel, early, n_rows, False),
        in_specs=[smem] + [vmem] * (len(flat(early)) + 1),
        scratch_shapes=rows_of(len(early) * HI),
    )(order, *flat(early), pre_grad)
    message = lambda n: shape((n, capacity + EXTRA, width), bf16)
    def begin(d, h):
        return pl.pallas_call(
            functools.partial(first_kernel, d, h),
            in_specs=[smem, vmem, vmem, hbm],
            out_specs=vmem,
            out_shape=message(1),
            scratch_shapes=rows_of(1),
            compiler_params=params,
            cost_estimate=cost(macs, 1 << 20),
        )(order, pre_grad, gate_mine, w_first)

    def carry_on(d, only, came, total):
        return pl.pallas_call(
            functools.partial(pass_kernel, d, only),
            in_specs=[smem, vmem, vmem, vmem, hbm],
            out_specs=[vmem, vmem],
            out_shape=(message(HI), shape((EXTRA, width), f32)),
            scratch_shapes=rows_of(HI),
            compiler_params=params,
            cost_estimate=cost(2 * macs, 1 << 20),
        )(order, came, pre_grad, total, w_first)

    from_left, from_right = right(begin(far, 0)), left(begin(far, 1))
    total_left, total_right = gate_mine, jnp.zeros_like(gate_mine)
    for d in range(far - 1, 0, -1):
        start = d == far - 1
        if d == 1:
            from_left, grad_down = lax.optimization_barrier((from_left, grad_down))
        go_right, total_left = carry_on(d, 0 if start else None, from_left, total_left)
        go_left, total_right = carry_on(-d, 1 if start else None, from_right, total_right)
        from_left, from_right = right(go_right), left(go_left)
    from_left, up_early = lax.optimization_barrier((from_left, up_early))
    grad_up = up_call(
        functools.partial(up_kernel, late, n_rows, True),
        in_specs=[smem] + [vmem] * (len(flat(late)) + 1) + [hbm],
        input_output_aliases={len(flat(late)) + 2: 0},
        scratch_shapes=rows_of(len(late) * HI),
    )(order, *flat(late), pre_grad, up_early)
    n_gate = capacity // width
    summed, gate_half = pl.pallas_call(
        last_kernel,
        in_specs=[smem, vmem, vmem, vmem, vmem, vmem, hbm],
        out_specs=[vmem, vmem],
        out_shape=(shape((HI, capacity, width), bf16), shape((n_gate, width), f32)),
        scratch_shapes=rows_of(HI),
        compiler_params=params,
        cost_estimate=cost(2 * macs, 2 << 20),
    )(order, from_left, from_right, pre_grad, total_left, total_right, w_first)
    gate_total = gate_half + lax.ppermute(gate_half, "hi", [(0, 1), (1, 0)])
    returned = lax.all_to_all(
        summed.reshape(HI * n_experts, n_slots, width), ("hi", "ep"), 0, 0, tiled=True
    ).reshape(HI, capacity, width)

    grad_tokens = pl.pallas_call(
        combine_kernel,
        out_shape=shape((n_tokens, width), bf16),
        compiler_params=params,
    )(selector, returned)
    return grad_tokens, grad_up[None], grad_down[None], gate_total.reshape(1, capacity)


def solution(mesh):
    n_ep, n_et = mesh.devices.shape
    fine = Mesh(mesh.devices.reshape(n_ep, HI, n_et // HI), ("ep", "hi", "row"))
    et = ("hi", "row")
    in_specs = (
        P("ep", et),
        P("ep", et),
        P("ep", None, et),
        P("ep", et, None),
        P("ep", None, et),
        P("ep", None),
        P("ep", None, None),
        P("ep", None),
    )
    out_specs = (P("ep", et), P("ep", None, et), P("ep", et, None), P("ep", None))
    return jax.shard_map(
        per_device, mesh=fine, in_specs=in_specs, out_specs=out_specs, check_vma=False
    )
```

time: 191 us -> 169 us (0.88)
  waiting for transfers between devices: 98.1 us -> 32.1 us
  starting transfers between devices: 16.6 us -> 73.9 us
  between operations: 14.1 us -> 1.13 us
    ppermute x0 -> x17, starting transfers between devices: none -> 59.6 us  [the longest x8 39 us: left(): lax.ppermute(a, 'row', [(i, (i - 1) % n_rows) for i in range(n_rows)])]
    all_gather x1 -> x0, waiting for transfers between devices: 52.7 us -> none  [per_device(): full = lax.all_gather(arrived, 'row', axis=0, tiled=False)]
    all_to_all x2 -> x1, waiting for transfers between devices: 45.4 us -> 4.65 us  [per_device(): lax.all_to_all(summed.reshape(HI * n_experts, n_slots, width), ('hi', 'ep...]
    ppermute x0 -> x17, waiting for transfers between devices: none -> 27.4 us  [the longest x8 19.6 us: left(): lax.ppermute(a, 'row', [(i, (i - 1) % n_rows) for i in range(n_rows)])]
    all_to_all x2 -> x1, starting transfers between devices: 16.6 us -> 14.4 us  [per_device(): lax.all_to_all(summed.reshape(HI * n_experts, n_slots, width), ('hi', 'ep...]
    pallas_call x4 -> x16, Pallas kernels: 22.9 us -> 23.5 us  [the longest x6 6 us: carry_on(): pl.pallas_call(functools.partial(pass_kernel, d, only), in_specs=[smem, v...]
  transfers between devices with their start and end apart: 3 -> 18, of which waited for: 3 -> 8; matrix products, arithmetic and copies ran while one was open for 1% -> 0% of each run, Pallas kernels for 7% -> 11%
where the time goes in v2:
time: 169 us; the launch traced here: 168 us
  starting transfers between devices  73.9 us (44%)
  blocking collectives  32.2 us (19%)
  waiting for transfers between devices  32.1 us (19%)
  Pallas kernels  25.5 us (15%)
  local copies, waits for them, and re-layouts  2.14 us (1%)
    ppermute x8, starting transfers between devices, left(): lax.ppermute(a, 'row', [(i, (i - 1) % n_rows) for i in range(n_rows)])  39 us
    all_to_all x1, blocking collectives, per_device(): lax.all_to_all(picked.reshape(HI * n_experts, n_slots, 2 * width), ('hi',...  32.2 us
    ppermute x8, waiting for transfers between devices, left(): lax.ppermute(a, 'row', [(i, (i - 1) % n_rows) for i in range(n_rows)])  19.6 us
    ppermute x8, starting transfers between devices, right(): lax.ppermute(a, 'row', [(i, (i + 1) % n_rows) for i in range(n_rows)])  15.5 us
    all_to_all x1, starting transfers between devices, per_device(): lax.all_to_all(summed.reshape(HI * n_experts, n_slots, width), ('hi', 'ep...  14.4 us
    ppermute x8, waiting for transfers between devices, right(): lax.ppermute(a, 'row', [(i, (i + 1) % n_rows) for i in range(n_rows)])  7.81 us
    pallas_call x6, Pallas kernels, carry_on(): pl.pallas_call(functools.partial(pass_kernel, d, only), in_specs=[smem, v...  6 us
    ppermute x1, starting transfers between devices, per_device(): gate_total = gate_half + lax.ppermute(gate_half, 'hi', [(0, 1), (1, 0)])  5.03 us
  transfers between devices with their start and end apart: 18, of which 8 were waited for; matrix products, arithmetic and copies ran while one was open for 0% of the time, Pallas kernels for 11%

profile of v2, /device:TPU:1, one launch (start us, length us, event | category | flops | bytes accessed | tf_op | source)
XLA Modules:
  0.0 167.6 jit_solution(4467338898242448765)
XLA Ops:
  0.6 2.0 %shard_map.111 = (bf16[512,256]{1,0:T(8,128)(2,1)}, bf16[2,512,256]{2,1,0:T(8,128)(2,1)}) custom-call(s32[16,32]{1,0:T(8,128)} %bitcast.37, s32[1,32]{1,0:T(1,128)} %counts_ref.1, bf16[256,128]{1,0:T(8,128)(2,1)} %tokens_ref.1, bf16[256,128]{1,0:T(8,128)(2,1)} %cotangent_ref.1), custom_call_target="tpu_custom_call" | custom-call | tf_op jit(solution)/shard_map/pallas_call | solution.py:271
  2.6 32.2 %all_to_all.10 = bf16[64,16,256]{2,1,0:T(8,128)(2,1)S(1)} all-to-all(bf16[64,16,256]{2,1,0:T(8,128)(2,1)} %bitcast.36), channel_id=1, replica_groups=mesh['ep'=32,'hi'=2,'row'=8] {'hi','ep'}, dimensions={0} | all-to-all | bytes 1048576 | tf_op jit(solution)/shard_map/all_to_all | solution.py:278
  34.8 5.1 %collective-permute-start.3 = (bf16[2,512,256]{2,1,0:T(8,128)(2,1)S(1)}, bf16[2,512,256]{2,1,0:T(8,128)(2,1)S(1)}, u32[]{:S(2)}, u32[]{:S(2)}) collective-permute-start(bf16[2,512,256]{2,1,0:T(8,128)(2,1)S(1)} %bitcast.23), channel_id=1, source_target_pairs={{0,7},{1,0},{2,1},{3,2},{4,3},{5,4},{6,5},{7,6},{8,15},{9,8},{10,9... | collective-permute-start | bytes 1572872 | tf_op jit(solution)/shard_map/ppermute | solution.py:262
  39.9 1.9 %collective-permute-start = (bf16[2,512,256]{2,1,0:T(8,128)(2,1)S(1)}, bf16[2,512,256]{2,1,0:T(8,128)(2,1)S(1)}, u32[]{:S(2)}, u32[]{:S(2)}) collective-permute-start(bf16[2,512,256]{2,1,0:T(8,128)(2,1)S(1)} %bitcast.24), channel_id=1, source_target_pairs={{0,1},{1,2},{2,3},{3,4},{4,5},{5,6},{6,7},{7,0},{8,9},{9,10},{10,1... | collective-permute-start | bytes 1572872 | tf_op jit(solution)/shard_map/ppermute | solution.py:259
  41.8 9.0 %collective-permute-done.3.refs_2_ = bf16[2,512,256]{2,1,0:T(8,128)(2,1)S(1)} collective-permute-done((bf16[2,512,256]{2,1,0:T(8,128)(2,1)S(1)}, bf16[2,512,256]{2,1,0:T(8,128)(2,1)S(1)}, u32[]{:S(2)}, u32[]{:S(2)}) %collective-permute-start.3) | collective-permute-done | bytes 524320 | tf_op jit(solution)/shard_map/ppermute | solution.py:262
  50.9 5.3 %collective-permute-start.4 = (bf16[2,512,256]{2,1,0:T(8,128)(2,1)S(1)}, bf16[2,512,256]{2,1,0:T(8,128)(2,1)S(1)}, u32[]{:S(2)}, u32[]{:S(2)}) collective-permute-start(bf16[2,512,256]{2,1,0:T(8,128)(2,1)S(1)} %collective-permute-done.3.refs_2_), channel_id=1, source_target_pairs={{0,7},{1,0},{2,1},{3,2},{4,3},{5,4},{6,5},{7,6},{8,15},{9,8},{10,9... | collective-permute-start | bytes 1572872 | tf_op jit(solution)/shard_map/ppermute | solution.py:262
  56.2 0.0 collective-permute-done.refs_1_
  56.2 1.9 %collective-permute-start.1 = (bf16[2,512,256]{2,1,0:T(8,128)(2,1)S(1)}, bf16[2,512,256]{2,1,0:T(8,128)(2,1)}, u32[]{:S(2)}, u32[]{:S(2)}) collective-permute-start(bf16[2,512,256]{2,1,0:T(8,128)(2,1)S(1)} %collective-permute-done.refs_1_), channel_id=1, source_target_pairs={{0,1},{1,2},{2,3},{3,4},{4,5},{5,6},{6,7},{7,0},{8,9},{9,10},{10,1... | collective-permute-start | bytes 1572872 | tf_op jit(solution)/shard_map/ppermute | solution.py:259
  58.1 8.1 %collective-permute-done.4.refs_4_ = bf16[2,512,256]{2,1,0:T(8,128)(2,1)S(1)} collective-permute-done((bf16[2,512,256]{2,1,0:T(8,128)(2,1)S(1)}, bf16[2,512,256]{2,1,0:T(8,128)(2,1)S(1)}, u32[]{:S(2)}, u32[]{:S(2)}) %collective-permute-start.4) | collective-permute-done | bytes 524320 | tf_op jit(solution)/shard_map/ppermute | solution.py:262
  66.2 5.3 %collective-permute-start.5 = (bf16[2,512,256]{2,1,0:T(8,128)(2,1)S(1)}, bf16[2,512,256]{2,1,0:T(8,128)(2,1)S(1)}, u32[]{:S(2)}, u32[]{:S(2)}) collective-permute-start(bf16[2,512,256]{2,1,0:T(8,128)(2,1)S(1)} %collective-permute-done.4.refs_4_), channel_id=1, source_target_pairs={{0,7},{1,0},{2,1},{3,2},{4,3},{5,4},{6,5},{7,6},{8,15},{9,8},{10,9... | collective-permute-start | bytes 1572872 | tf_op jit(solution)/shard_map/ppermute | solution.py:262
  71.5 0.0 collective-permute-done.1.refs_3_
  71.5 1.9 %collective-permute-start.2 = (bf16[2,512,256]{2,1,0:T(8,128)(2,1)}, bf16[2,512,256]{2,1,0:T(8,128)(2,1)S(1)}, u32[]{:S(2)}, u32[]{:S(2)}) collective-permute-start(bf16[2,512,256]{2,1,0:T(8,128)(2,1)} %collective-permute-done.1.refs_3_), channel_id=1, source_target_pairs={{0,1},{1,2},{2,3},{3,4},{4,5},{5,6},{6,7},{7,0},{8,9},{9,10},{10,1... | collective-permute-start | bytes 1572872 | tf_op jit(solution)/shard_map/ppermute | solution.py:259
  73.5 0.0 copy-start.10
  73.5 0.7 copy-done.10
  74.2 0.1 copy.14.refs_6_.refs_7_.refs_5_
  74.3 0.0 copy-start.2
  74.3 0.1 pad_add_fusion.order_ref
  74.4 1.2 copy-done.1
  75.7 2.6 %shard_map.112.refs_5_ = f32[512,256]{1,0:T(8,128)S(1)} custom-call(s32[16]{0:T(128)S(1)} %pad_add_fusion.order_ref, bf16[2,512,256]{2,1,0:T(8,128)(2,1)S(1)} %bitcast.25, bf16[2,512,256]{2,1,0:T(8,128)(2,1)S(1)} %collective-permute-done.refs_1_, bf16[2,512,256]{2,1,0:T(8,128)(2,1)S(1)} %collective-permute-done.3.refs_2_, ...), custom_call_target="tpu_custom_call" | custom-call | flops 335544320 | bytes 4194304 | tf_op jit(solution)/shard_map/pallas_call | solution.py:293
  78.3 2.5 %shard_map.113.refs_6_ = bf16[256,2048]{1,0:T(8,128)(2,1)} custom-call(s32[16]{0:T(128)S(1)} %pad_add_fusion.order_ref, bf16[2,512,256]{2,1,0:T(8,128)(2,1)S(1)} %bitcast.26, bf16[2,512,256]{2,1,0:T(8,128)(2,1)S(1)} %collective-permute-done.refs_1_, bf16[2,512,256]{2,1,0:T(8,128)(2,1)S(1)} %collective-permute-done.3.refs_2_, ...), custom_call_target="tpu_custom_call" | custom-call | flops 335544320 | bytes 4194304 | tf_op jit(solution)/shard_map/pallas_call | solution.py:302
  80.8 0.0 collective-permute-done.5.refs_0_
  80.8 5.1 %collective-permute-done.2.refs_1_ = bf16[2,512,256]{2,1,0:T(8,128)(2,1)S(1)} collective-permute-done((bf16[2,512,256]{2,1,0:T(8,128)(2,1)}, bf16[2,512,256]{2,1,0:T(8,128)(2,1)S(1)}, u32[]{:S(2)}, u32[]{:S(2)}) %collective-permute-start.2) | collective-permute-done | bytes 524320 | tf_op jit(solution)/shard_map/ppermute | solution.py:259
  86.0 0.0 copy-start.3
  86.0 0.0 copy-start
  86.0 2.1 %collective-permute-start.6 = (bf16[1,512,256]{2,1,0:T(8,128)(2,1)S(1)}, bf16[1,512,256]{2,1,0:T(8,128)(2,1)S(1)}, u32[]{:S(2)}, u32[]{:S(2)}) collective-permute-start(bf16[1,512,256]{2,1,0:T(8,128)(2,1)S(1)} %slice.6), channel_id=1, source_target_pairs={{0,1},{1,2},{2,3},{3,4},{4,5},{5,6},{6,7},{7,0},{8,9},{9,10},{10,1... | collective-permute-start | bytes 786440 | tf_op jit(solution)/shard_map/ppermute | solution.py:259
  88.1 4.6 %collective-permute-start.7 = (bf16[1,512,256]{2,1,0:T(8,128)(2,1)S(1)}, bf16[1,512,256]{2,1,0:T(8,128)(2,1)S(1)}, u32[]{:S(2)}, u32[]{:S(2)}) collective-permute-start(bf16[1,512,256]{2,1,0:T(8,128)(2,1)S(1)} %slice.7), channel_id=1, source_target_pairs={{0,7},{1,0},{2,1},{3,2},{4,3},{5,4},{6,5},{7,6},{8,15},{9,8},{10,9... | collective-permute-start | bytes 786440 | tf_op jit(solution)/shard_map/ppermute | solution.py:262
  92.6 1.8 %collective-permute-done.6.refs_2_ = bf16[1,512,256]{2,1,0:T(8,128)(2,1)S(1)} collective-permute-done((bf16[1,512,256]{2,1,0:T(8,128)(2,1)S(1)}, bf16[1,512,256]{2,1,0:T(8,128)(2,1)S(1)}, u32[]{:S(2)}, u32[]{:S(2)}) %collective-permute-start.6) | collective-permute-done | bytes 262176 | tf_op jit(solution)/shard_map/ppermute | solution.py:259
  94.5 1.5 collective-permute-done.7.refs_3_
  95.9 2.1 %shard_map.114 = (bf16[512,256]{1,0:T(8,128)(2,1)S(1)}, f32[16,128]{1,0:T(8,128)S(1)}) custom-call(s32[16]{0:T(128)S(1)} %pad_add_fusion.order_ref, bf16[2,512,256]{2,1,0:T(8,128)(2,1)S(1)} %collective-permute-done.5.refs_0_, bf16[2,512,256]{2,1,0:T(8,128)(2,1)S(1)} %collective-permute-done.2.refs_1_, ...), custom_call_target="tpu_custom_call" | custom-call | flops 201326592 | bytes 3145728 | tf_op jit(solution)/shard_map/pallas_call | solution.py:316
  98.1 0.9 shard_map.115
  99.0 1.9 %collective-permute-start.8 = (bf16[1,528,128]{2,1,0:T(8,128)(2,1)S(1)}, bf16[1,528,128]{2,1,0:T(8,128)(2,1)S(1)}, u32[]{:S(2)}, u32[]{:S(2)}) collective-permute-start(bf16[1,528,128]{2,1,0:T(8,128)(2,1)S(1)} %shard_map.115), channel_id=1, source_target_pairs={{0,1},{1,2},{2,3},{3,4},{4,5},{5,6},{6,7},{7,0},{8,9},{9,10},{10,1... | collective-permute-start | bytes 405512 | tf_op jit(solution)/shard_map/ppermute | solution.py:259
  100.9 0.9 shard_map.121
  101.8 5.0 %collective-permute-start.12 = (bf16[1,528,128]{2,1,0:T(8,128)(2,1)S(1)}, bf16[1,528,128]{2,1,0:T(8,128)(2,1)S(1)}, u32[]{:S(2)}, u32[]{:S(2)}) collective-permute-start(bf16[1,528,128]{2,1,0:T(8,128)(2,1)S(1)} %shard_map.121), channel_id=1, source_target_pairs={{0,7},{1,0},{2,1},{3,2},{4,3},{5,4},{6,5},{7,6},{8,15},{9,8},{10,9... | collective-permute-start | bytes 405512 | tf_op jit(solution)/shard_map/ppermute | solution.py:262
  106.8 0.0 collective-permute-done.8.came
  106.8 1.0 shard_map.116
  107.8 1.9 %collective-permute-start.9 = (bf16[2,528,128]{2,1,0:T(8,128)(2,1)S(1)}, bf16[2,528,128]{2,1,0:T(8,128)(2,1)S(1)}, u32[]{:S(2)}, u32[]{:S(2)}) collective-permute-start(bf16[2,528,128]{2,1,0:T(8,128)(2,1)S(1)} %get-tuple-element.37), channel_id=1, source_target_pairs={{0,1},{1,2},{2,3},{3,4},{4,5},{5,6},{6,7},{7,0},{8,9},{9,10},{10,1... | collective-permute-start | bytes 811016 | tf_op jit(solution)/shard_map/ppermute | solution.py:259
  109.7 0.0 collective-permute-done.12.came
  109.8 1.0 shard_map.122
  110.8 4.6 %collective-permute-start.13 = (bf16[2,528,128]{2,1,0:T(8,128)(2,1)S(1)}, bf16[2,528,128]{2,1,0:T(8,128)(2,1)S(1)}, u32[]{:S(2)}, u32[]{:S(2)}) collective-permute-start(bf16[2,528,128]{2,1,0:T(8,128)(2,1)S(1)} %get-tuple-element.45), channel_id=1, source_target_pairs={{0,7},{1,0},{2,1},{3,2},{4,3},{5,4},{6,5},{7,6},{8,15},{9,8},{10,9... | collective-permute-start | bytes 811016 | tf_op jit(solution)/shard_map/ppermute | solution.py:262
  115.4 0.9 collective-permute-done.9.came
  116.2 1.0 shard_map.117
  117.2 1.9 %collective-permute-start.10 = (bf16[2,528,128]{2,1,0:T(8,128)(2,1)S(1)}, bf16[2,528,128]{2,1,0:T(8,128)(2,1)S(1)}, u32[]{:S(2)}, u32[]{:S(2)}) collective-permute-start(bf16[2,528,128]{2,1,0:T(8,128)(2,1)S(1)} %get-tuple-element.39), channel_id=1, source_target_pairs={{0,1},{1,2},{2,3},{3,4},{4,5},{5,6},{6,7},{7,0},{8,9},{9,10},{10,1... | collective-permute-start | bytes 811016 | tf_op jit(solution)/shard_map/ppermute | solution.py:259
  119.2 0.0 collective-permute-done.13.came
  119.2 1.0 shard_map.123
  120.2 4.6 %collective-permute-start.14 = (bf16[2,528,128]{2,1,0:T(8,128)(2,1)S(1)}, bf16[2,528,128]{2,1,0:T(8,128)(2,1)S(1)}, u32[]{:S(2)}, u32[]{:S(2)}) collective-permute-start(bf16[2,528,128]{2,1,0:T(8,128)(2,1)S(1)} %get-tuple-element.47), channel_id=1, source_target_pairs={{0,7},{1,0},{2,1},{3,2},{4,3},{5,4},{6,5},{7,6},{8,15},{9,8},{10,9... | collective-permute-start | bytes 811016 | tf_op jit(solution)/shard_map/ppermute | solution.py:262
  124.8 1.9 %shard_map.118 = bf16[256,2048]{1,0:T(8,128)(2,1)} custom-call(s32[16]{0:T(128)S(1)} %pad_add_fusion.order_ref, bf16[2,512,256]{2,1,0:T(8,128)(2,1)S(1)} %collective-permute-done.5.refs_0_, bf16[2,512,256]{2,1,0:T(8,128)(2,1)S(1)} %collective-permute-done.2.refs_1_, ...), custom_call_target="tpu_custom_call", output_to_operand_aliasing={{}: (7, {})} | custom-call | flops 201326592 | bytes 3145728 | tf_op jit(solution)/shard_map/pallas_call | solution.py:326
  126.7 0.0 collective-permute-done.10.came
  126.7 1.0 shard_map.119
  127.7 1.9 %collective-permute-start.11 = (bf16[2,528,128]{2,1,0:T(8,128)(2,1)S(1)}, bf16[2,528,128]{2,1,0:T(8,128)(2,1)S(1)}, u32[]{:S(2)}, u32[]{:S(2)}) collective-permute-start(bf16[2,528,128]{2,1,0:T(8,128)(2,1)S(1)} %get-tuple-element.43), channel_id=1, source_target_pairs={{0,1},{1,2},{2,3},{3,4},{4,5},{5,6},{6,7},{7,0},{8,9},{9,10},{10,1... | collective-permute-start | bytes 811016 | tf_op jit(solution)/shard_map/ppermute | solution.py:259
  129.6 0.0 collective-permute-done.14.came
  129.6 1.0 shard_map.124
  130.6 4.6 %collective-permute-start.15 = (bf16[2,528,128]{2,1,0:T(8,128)(2,1)S(1)}, bf16[2,528,128]{2,1,0:T(8,128)(2,1)S(1)}, u32[]{:S(2)}, u32[]{:S(2)}) collective-permute-start(bf16[2,528,128]{2,1,0:T(8,128)(2,1)S(1)} %get-tuple-element.49), channel_id=1, source_target_pairs={{0,7},{1,0},{2,1},{3,2},{4,3},{5,4},{6,5},{7,6},{8,15},{9,8},{10,9... | collective-permute-start | bytes 811016 | tf_op jit(solution)/shard_map/ppermute | solution.py:262
  135.2 2.4 %shard_map.120.refs_5_ = bf16[2048,256]{1,0:T(8,128)(2,1)} custom-call(s32[16]{0:T(128)S(1)} %pad_add_fusion.order_ref, bf16[2,512,256]{2,1,0:T(8,128)(2,1)S(1)} %bitcast.27, bf16[2,512,256]{2,1,0:T(8,128)(2,1)S(1)} %collective-permute-done.refs_1_, bf16[2,512,256]{2,1,0:T(8,128)(2,1)S(1)} %collective-permute-done.3.refs_2_, ...), custom_call_target="tpu_custom_call" | custom-call | flops 268435456 | bytes 4194304 | tf_op jit(solution)/shard_map/pallas_call | solution.py:343
  137.6 0.0 collective-permute-done.11.from_left
  137.6 1.0 collective-permute-done.15.from_right
  138.6 1.7 %shard_map.125 = (bf16[2,512,128]{2,1,0:T(8,128)(2,1)}, f32[4,128]{1,0:T(4,128)S(1)}) custom-call(s32[16]{0:T(128)S(1)} %pad_add_fusion.order_ref, bf16[2,528,128]{2,1,0:T(8,128)(2,1)S(1)} %collective-permute-done.11.from_left, bf16[2,528,128]{2,1,0:T(8,128)(2,1)S(1)} %collective-permute-done.15.from_right, ...), custom_call_target="tpu_custom_call" | custom-call | flops 67108864 | bytes 2097152 | tf_op jit(solution)/shard_map/pallas_call | solution.py:388
  140.3 14.4 %all-to-all-start.1 = ((bf16[64,16,128]{2,1,0:T(8,128)(2,1)}), bf16[64,16,128]{2,1,0:T(8,128)(2,1)S(1)}, u32[]{:S(2)}, u32[]{:S(2)}) async-start(bf16[64,16,128]{2,1,0:T(8,128)(2,1)} %bitcast.8), calls=%async_computation.1 | async-start | bytes 524288 | tf_op jit(solution)/shard_map/all_to_all | solution.py:398
  154.7 0.0 copy-start.9
  154.7 5.0 %collective-permute-start.16 = (f32[4,128]{1,0:T(4,128)S(1)}, f32[4,128]{1,0:T(4,128)S(1)}, u32[]{:S(2)}, u32[]{:S(2)}) collective-permute-start(f32[4,128]{1,0:T(4,128)S(1)} %get-tuple-element.55), channel_id=1, source_target_pairs={{0,8},{8,0},{1,9},{9,1},{2,10},{10,2},{3,11},{11,3},{4,12},{12,4},... | collective-permute-start | bytes 6152 | tf_op jit(solution)/shard_map/ppermute | solution.py:397
  159.8 1.7 %shard_map.127 = bf16[2048,256]{1,0:T(8,128)(2,1)} custom-call(s32[16]{0:T(128)S(1)} %pad_add_fusion.order_ref, bf16[2,512,256]{2,1,0:T(8,128)(2,1)S(1)} %collective-permute-done.5.refs_0_, bf16[2,512,256]{2,1,0:T(8,128)(2,1)S(1)} %collective-permute-done.2.refs_1_, bf16[1,512,256]{2,1,0:T(8,128)(2,1)S(1)} %copy-done.6, ...), custom_call_target="tpu_custom_call", output_to_operand_aliasing={{}: (6, {})} | custom-call | flops 268435456 | bytes 4194304 | tf_op jit(solution)/shard_map/pallas_call | solution.py:381
  161.5 0.0 collective-permute-done.16
  161.5 0.6 add.22
  162.1 4.6 %all-to-all-done.1 = bf16[64,16,128]{2,1,0:T(8,128)(2,1)S(1)} async-done(((bf16[64,16,128]{2,1,0:T(8,128)(2,1)}), bf16[64,16,128]{2,1,0:T(8,128)(2,1)S(1)}, u32[]{:S(2)}, u32[]{:S(2)}) %all-to-all-start.1) | async-done | bytes 262176 | tf_op jit(solution)/shard_map/all_to_all | solution.py:398
  166.7 0.9 shard_map.126
  (19 shorter events, 0.1 us)
Async XLA Ops:
  34.8 16.1 %collective-permute-start.3 = (bf16[2,512,256]{2,1,0:T(8,128)(2,1)S(1)}, bf16[2,512,256]{2,1,0:T(8,128)(2,1)S(1)}, u32[]{:S(2)}, u32[]{:S(2)}) collective-permute-start(bf16[2,512,256]{2,1,0:T(8,128)(2,1)S(1)} %bitcast.23), channel_id=1, source_target_pairs={{0,7},{1,0},{2,1},{3,2},{4,3},{5,4},{6,5},{7,6},{8,15},{9,8},{10,9... | collective-permute-start | bytes 1572872 | tf_op jit(solution)/shard_map/ppermute | solution.py:262
  39.9 16.3 %collective-permute-start = (bf16[2,512,256]{2,1,0:T(8,128)(2,1)S(1)}, bf16[2,512,256]{2,1,0:T(8,128)(2,1)S(1)}, u32[]{:S(2)}, u32[]{:S(2)}) collective-permute-start(bf16[2,512,256]{2,1,0:T(8,128)(2,1)S(1)} %bitcast.24), channel_id=1, source_target_pairs={{0,1},{1,2},{2,3},{3,4},{4,5},{5,6},{6,7},{7,0},{8,9},{9,10},{10,1... | collective-permute-start | bytes 1572872 | tf_op jit(solution)/shard_map/ppermute | solution.py:259
  50.9 15.4 %collective-permute-start.4 = (bf16[2,512,256]{2,1,0:T(8,128)(2,1)S(1)}, bf16[2,512,256]{2,1,0:T(8,128)(2,1)S(1)}, u32[]{:S(2)}, u32[]{:S(2)}) collective-permute-start(bf16[2,512,256]{2,1,0:T(8,128)(2,1)S(1)} %collective-permute-done.3.refs_2_), channel_id=1, source_target_pairs={{0,7},{1,0},{2,1},{3,2},{4,3},{5,4},{6,5},{7,6},{8,15},{9,8},{10,9... | collective-permute-start | bytes 1572872 | tf_op jit(solution)/shard_map/ppermute | solution.py:262
  56.2 15.4 %collective-permute-start.1 = (bf16[2,512,256]{2,1,0:T(8,128)(2,1)S(1)}, bf16[2,512,256]{2,1,0:T(8,128)(2,1)}, u32[]{:S(2)}, u32[]{:S(2)}) collective-permute-start(bf16[2,512,256]{2,1,0:T(8,128)(2,1)S(1)} %collective-permute-done.refs_1_), channel_id=1, source_target_pairs={{0,1},{1,2},{2,3},{3,4},{4,5},{5,6},{6,7},{7,0},{8,9},{9,10},{10,1... | collective-permute-start | bytes 1572872 | tf_op jit(solution)/shard_map/ppermute | solution.py:259
  66.2 14.6 %collective-permute-start.5 = (bf16[2,512,256]{2,1,0:T(8,128)(2,1)S(1)}, bf16[2,512,256]{2,1,0:T(8,128)(2,1)S(1)}, u32[]{:S(2)}, u32[]{:S(2)}) collective-permute-start(bf16[2,512,256]{2,1,0:T(8,128)(2,1)S(1)} %collective-permute-done.4.refs_4_), channel_id=1, source_target_pairs={{0,7},{1,0},{2,1},{3,2},{4,3},{5,4},{6,5},{7,6},{8,15},{9,8},{10,9... | collective-permute-start | bytes 1572872 | tf_op jit(solution)/shard_map/ppermute | solution.py:262
  71.5 14.4 %collective-permute-start.2 = (bf16[2,512,256]{2,1,0:T(8,128)(2,1)}, bf16[2,512,256]{2,1,0:T(8,128)(2,1)S(1)}, u32[]{:S(2)}, u32[]{:S(2)}) collective-permute-start(bf16[2,512,256]{2,1,0:T(8,128)(2,1)} %collective-permute-done.1.refs_3_), channel_id=1, source_target_pairs={{0,1},{1,2},{2,3},{3,4},{4,5},{5,6},{6,7},{7,0},{8,9},{9,10},{10,1... | collective-permute-start | bytes 1572872 | tf_op jit(solution)/shard_map/ppermute | solution.py:259
  73.5 0.7 copy-start.10
  74.3 3.9 %copy-start.2 = (f32[512,1]{1,0:T(8,128)}, f32[512,1]{1,0:T(8,128)S(1)}, u32[]{:S(2)}) copy-start(f32[512,1]{1,0:T(8,128)S(1)} %copy.14.refs_6_.refs_7_.refs_5_) | copy-start | bytes 6148
  74.4 1.2 copy-start.1
  75.7 2.6 %copy-start.4 = (bf16[1,512,256]{2,1,0:T(8,128)(2,1)S(1)}, bf16[1,512,256]{2,1,0:T(8,128)(2,1)}, u32[]{:S(2)}) copy-start(bf16[1,512,256]{2,1,0:T(8,128)(2,1)} %param.12) | copy-start | bytes 786436
  86.0 10.0 %copy-start.3 = (f32[512,1]{1,0:T(8,128)S(1)}, f32[512,1]{1,0:T(8,128)}, u32[]{:S(2)}) copy-start(f32[512,1]{1,0:T(8,128)} %copy-done.2) | copy-start | bytes 6148
  86.0 12.1 %copy-start = (bf16[1,2048,256]{2,1,0:T(8,128)(2,1)S(1)}, bf16[1,2048,256]{2,1,0:T(8,128)(2,1)}, u32[]{:S(2)}) copy-start(bf16[1,2048,256]{2,1,0:T(8,128)(2,1)} %param.10) | copy-start | bytes 3145732
  86.0 8.5 %collective-permute-start.6 = (bf16[1,512,256]{2,1,0:T(8,128)(2,1)S(1)}, bf16[1,512,256]{2,1,0:T(8,128)(2,1)S(1)}, u32[]{:S(2)}, u32[]{:S(2)}) collective-permute-start(bf16[1,512,256]{2,1,0:T(8,128)(2,1)S(1)} %slice.6), channel_id=1, source_target_pairs={{0,1},{1,2},{2,3},{3,4},{4,5},{5,6},{6,7},{7,0},{8,9},{9,10},{10,1... | collective-permute-start | bytes 786440 | tf_op jit(solution)/shard_map/ppermute | solution.py:259
  88.1 7.9 %collective-permute-start.7 = (bf16[1,512,256]{2,1,0:T(8,128)(2,1)S(1)}, bf16[1,512,256]{2,1,0:T(8,128)(2,1)S(1)}, u32[]{:S(2)}, u32[]{:S(2)}) collective-permute-start(bf16[1,512,256]{2,1,0:T(8,128)(2,1)S(1)} %slice.7), channel_id=1, source_target_pairs={{0,7},{1,0},{2,1},{3,2},{4,3},{5,4},{6,5},{7,6},{8,15},{9,8},{10,9... | collective-permute-start | bytes 786440 | tf_op jit(solution)/shard_map/ppermute | solution.py:262
  94.5 30.3 %copy-start.5 = (bf16[1,512,256]{2,1,0:T(8,128)(2,1)}, bf16[1,512,256]{2,1,0:T(8,128)(2,1)S(1)}, u32[]{:S(2)}) copy-start(bf16[1,512,256]{2,1,0:T(8,128)(2,1)S(1)} %collective-permute-done.6.refs_2_) | copy-start | bytes 786436
  95.9 28.9 %copy-start.7 = (bf16[1,512,256]{2,1,0:T(8,128)(2,1)}, bf16[1,512,256]{2,1,0:T(8,128)(2,1)S(1)}, u32[]{:S(2)}) copy-start(bf16[1,512,256]{2,1,0:T(8,128)(2,1)S(1)} %collective-permute-done.7.refs_3_) | copy-start | bytes 786436
  99.0 7.8 %collective-permute-start.8 = (bf16[1,528,128]{2,1,0:T(8,128)(2,1)S(1)}, bf16[1,528,128]{2,1,0:T(8,128)(2,1)S(1)}, u32[]{:S(2)}, u32[]{:S(2)}) collective-permute-start(bf16[1,528,128]{2,1,0:T(8,128)(2,1)S(1)} %shard_map.115), channel_id=1, source_target_pairs={{0,1},{1,2},{2,3},{3,4},{4,5},{5,6},{6,7},{7,0},{8,9},{9,10},{10,1... | collective-permute-start | bytes 405512 | tf_op jit(solution)/shard_map/ppermute | solution.py:259
  101.8 8.0 %collective-permute-start.12 = (bf16[1,528,128]{2,1,0:T(8,128)(2,1)S(1)}, bf16[1,528,128]{2,1,0:T(8,128)(2,1)S(1)}, u32[]{:S(2)}, u32[]{:S(2)}) collective-permute-start(bf16[1,528,128]{2,1,0:T(8,128)(2,1)S(1)} %shard_map.121), channel_id=1, source_target_pairs={{0,7},{1,0},{2,1},{3,2},{4,3},{5,4},{6,5},{7,6},{8,15},{9,8},{10,9... | collective-permute-start | bytes 405512 | tf_op jit(solution)/shard_map/ppermute | solution.py:262
  107.8 8.4 %collective-permute-start.9 = (bf16[2,528,128]{2,1,0:T(8,128)(2,1)S(1)}, bf16[2,528,128]{2,1,0:T(8,128)(2,1)S(1)}, u32[]{:S(2)}, u32[]{:S(2)}) collective-permute-start(bf16[2,528,128]{2,1,0:T(8,128)(2,1)S(1)} %get-tuple-element.37), channel_id=1, source_target_pairs={{0,1},{1,2},{2,3},{3,4},{4,5},{5,6},{6,7},{7,0},{8,9},{9,10},{10,1... | collective-permute-start | bytes 811016 | tf_op jit(solution)/shard_map/ppermute | solution.py:259
  110.8 8.4 %collective-permute-start.13 = (bf16[2,528,128]{2,1,0:T(8,128)(2,1)S(1)}, bf16[2,528,128]{2,1,0:T(8,128)(2,1)S(1)}, u32[]{:S(2)}, u32[]{:S(2)}) collective-permute-start(bf16[2,528,128]{2,1,0:T(8,128)(2,1)S(1)} %get-tuple-element.45), channel_id=1, source_target_pairs={{0,7},{1,0},{2,1},{3,2},{4,3},{5,4},{6,5},{7,6},{8,15},{9,8},{10,9... | collective-permute-start | bytes 811016 | tf_op jit(solution)/shard_map/ppermute | solution.py:262
  117.2 9.4 %collective-permute-start.10 = (bf16[2,528,128]{2,1,0:T(8,128)(2,1)S(1)}, bf16[2,528,128]{2,1,0:T(8,128)(2,1)S(1)}, u32[]{:S(2)}, u32[]{:S(2)}) collective-permute-start(bf16[2,528,128]{2,1,0:T(8,128)(2,1)S(1)} %get-tuple-element.39), channel_id=1, source_target_pairs={{0,1},{1,2},{2,3},{3,4},{4,5},{5,6},{6,7},{7,0},{8,9},{9,10},{10,1... | collective-permute-start | bytes 811016 | tf_op jit(solution)/shard_map/ppermute | solution.py:259
  120.2 9.4 %collective-permute-start.14 = (bf16[2,528,128]{2,1,0:T(8,128)(2,1)S(1)}, bf16[2,528,128]{2,1,0:T(8,128)(2,1)S(1)}, u32[]{:S(2)}, u32[]{:S(2)}) collective-permute-start(bf16[2,528,128]{2,1,0:T(8,128)(2,1)S(1)} %get-tuple-element.47), channel_id=1, source_target_pairs={{0,7},{1,0},{2,1},{3,2},{4,3},{5,4},{6,5},{7,6},{8,15},{9,8},{10,9... | collective-permute-start | bytes 811016 | tf_op jit(solution)/shard_map/ppermute | solution.py:262
  127.7 9.9 %collective-permute-start.11 = (bf16[2,528,128]{2,1,0:T(8,128)(2,1)S(1)}, bf16[2,528,128]{2,1,0:T(8,128)(2,1)S(1)}, u32[]{:S(2)}, u32[]{:S(2)}) collective-permute-start(bf16[2,528,128]{2,1,0:T(8,128)(2,1)S(1)} %get-tuple-element.43), channel_id=1, source_target_pairs={{0,1},{1,2},{2,3},{3,4},{4,5},{5,6},{6,7},{7,0},{8,9},{9,10},{10,1... | collective-permute-start | bytes 811016 | tf_op jit(solution)/shard_map/ppermute | solution.py:259
  130.6 8.0 %collective-permute-start.15 = (bf16[2,528,128]{2,1,0:T(8,128)(2,1)S(1)}, bf16[2,528,128]{2,1,0:T(8,128)(2,1)S(1)}, u32[]{:S(2)}, u32[]{:S(2)}) collective-permute-start(bf16[2,528,128]{2,1,0:T(8,128)(2,1)S(1)} %get-tuple-element.49), channel_id=1, source_target_pairs={{0,7},{1,0},{2,1},{3,2},{4,3},{5,4},{6,5},{7,6},{8,15},{9,8},{10,9... | collective-permute-start | bytes 811016 | tf_op jit(solution)/shard_map/ppermute | solution.py:262
  140.3 19.5 %copy-start.6 = (bf16[1,512,256]{2,1,0:T(8,128)(2,1)S(1)}, bf16[1,512,256]{2,1,0:T(8,128)(2,1)}, u32[]{:S(2)}) copy-start(bf16[1,512,256]{2,1,0:T(8,128)(2,1)} %copy-done.5) | copy-start | bytes 786436
  140.3 19.5 %copy-start.8 = (bf16[1,512,256]{2,1,0:T(8,128)(2,1)S(1)}, bf16[1,512,256]{2,1,0:T(8,128)(2,1)}, u32[]{:S(2)}) copy-start(bf16[1,512,256]{2,1,0:T(8,128)(2,1)} %copy-done.7) | copy-start | bytes 786436
  140.3 26.4 %all-to-all-start.1 = ((bf16[64,16,128]{2,1,0:T(8,128)(2,1)}), bf16[64,16,128]{2,1,0:T(8,128)(2,1)S(1)}, u32[]{:S(2)}, u32[]{:S(2)}) async-start(bf16[64,16,128]{2,1,0:T(8,128)(2,1)} %bitcast.8), calls=%async_computation.1 | async-start | bytes 524288 | tf_op jit(solution)/shard_map/all_to_all | solution.py:398
  154.7 12.0 %copy-start.9 = (bf16[512,256]{1,0:T(8,128)(2,1)S(1)}, bf16[512,256]{1,0:T(8,128)(2,1)}, u32[]{:S(2)}) copy-start(bf16[512,256]{1,0:T(8,128)(2,1)} %get-tuple-element.30.sel_ref) | copy-start | bytes 786436
  154.7 6.8 %collective-permute-start.16 = (f32[4,128]{1,0:T(4,128)S(1)}, f32[4,128]{1,0:T(4,128)S(1)}, u32[]{:S(2)}, u32[]{:S(2)}) collective-permute-start(f32[4,128]{1,0:T(4,128)S(1)} %get-tuple-element.55), channel_id=1, source_target_pairs={{0,8},{8,0},{1,9},{9,1},{2,10},{10,2},{3,11},{11,3},{4,12},{12,4},... | collective-permute-start | bytes 6152 | tf_op jit(solution)/shard_map/ppermute | solution.py:397

commit v3 on v2

--- a/solution.py
+++ b/solution.py
@@ -12,7 +12,7 @@
 NN = (((1,), (0,)), ((), ()))
 NT = (((1,), (1,)), ((), ()))
 TN = (((0,), (0,)), ((), ()))
-VMEM_LIMIT = 20 << 20
+VMEM_LIMIT = 12 << 20
 
 
 def dot32(a, b, dims=NN):
@@ -41,11 +41,20 @@
     return pl.multiple_of(order_ref[h * n_rows + d % n_rows] * 128, 128)
 
 
-def half_of(blocks, n, h, side):
-    width = blocks[0].shape[-1] // 2
-    if len(blocks) == 1:
-        return blocks[0][h, :, side * width : (side + 1) * width]
-    return blocks[h][0, :, side * width : (side + 1) * width]
+def y_of(blocks, h):
+    return blocks[0][2 * h] if len(blocks) == 1 else blocks[h][0]
+
+
+def pack_kernel(hi_ref, arrived_ref, out_ref):
+    width = out_ref.shape[-1]
+    out_ref[0] = arrived_ref[0, :, width:]
+    out_ref[1] = arrived_ref[hi_ref[0], :, :width]
+    out_ref[2] = arrived_ref[1, :, width:]
+
+
+def stack_kernel(*refs):
+    for k, ref in enumerate(refs[:-1]):
+        refs[-1][k] = ref[0]
 
 
 def grouped(refs, distances, n_rows):
@@ -86,7 +95,7 @@
         for h in range(HI):
             copies[k * HI + h].wait()
         pair = jnp.concatenate(
-            [half_of(groups[k], n_rows, h, 1) for h in range(HI)], axis=1
+            [y_of(groups[k], h) for h in range(HI)], axis=1
         )
         term = dot32(pair, down[:, k * HI * 128 : (k + 1) * HI * 128], NT)
         back = term if back is None else back + term
@@ -182,7 +191,7 @@
     copies = []
     for k, d in enumerate(distances):
         pair = jnp.concatenate(
-            [half_of(groups[k], n_rows, h, 1) for h in range(HI)], axis=1
+            [y_of(groups[k], h) for h in range(HI)], axis=1
         )
         scaled = (gate_ref[...] * pair.astype(jnp.float32)).astype(jnp.bfloat16)
         out[:, k * HI * 128 : (k + 1) * HI * 128] = dot32(hidden_t, scaled).astype(
@@ -201,17 +210,11 @@
         copy.wait()
 
 
-def up_kernel(distances, n_rows, more, order_ref, *refs):
-    groups, rest = grouped(refs, distances, n_rows)
-    if more:
-        pre_grad_ref, _, out_hbm, out, sems = rest
-    else:
-        pre_grad_ref, out_hbm, out, sems = rest
+def up_kernel(distances, more, order_ref, own_ref, other_ref, pre_grad_ref, *refs):
+    out_hbm, out, sems = refs[1:] if more else refs
     copies = []
     for k, d in enumerate(distances):
-        pair = jnp.concatenate(
-            [half_of(groups[k], n_rows, h, 0) for h in range(HI)], axis=1
-        )
+        pair = jnp.concatenate([own_ref[k], other_ref[k]], axis=1)
         out[k * HI * 128 : (k + 1) * HI * 128, :] = dot32(
             pair, pre_grad_ref[...], TN
         ).astype(jnp.bfloat16)
@@ -264,7 +267,7 @@
     hi, row = lax.axis_index("hi"), lax.axis_index("row")
     ahead_of = (row + jnp.arange(n_rows, dtype=jnp.int32)) % n_rows
     order = jnp.concatenate([h * n_rows + ahead_of for h in range(HI)])
-    del hi
+    order_x = jnp.concatenate([h * n_rows + ahead_of for h in (hi, 1 - hi)])
     gate_column = gates[0][:, None]
     pre, w_first, w_second = saved_pre[0], w_up[0], w_down[0]
 
@@ -279,11 +282,41 @@
         picked.reshape(HI * n_experts, n_slots, 2 * width), ("hi", "ep"), 0, 0, tiled=True
     ).reshape(HI, capacity, 2 * width)
 
-    blocks = {0: [arrived]}
-    behind = ahead = arrived
+    arrived, order, order_x, gate_column = lax.optimization_barrier(
+        (arrived, order, order_x, gate_column)
+    )
+    packed = pl.pallas_call(
+        pack_kernel,
+        in_specs=[smem, vmem],
+        out_specs=vmem,
+        out_shape=shape((HI + 1, capacity, width), bf16),
+        compiler_params=params,
+    )(hi[None], arrived)
+
+    def stacked(pieces):
+        return pl.pallas_call(
+            stack_kernel,
+            grid=(1,),
+            in_specs=[pl.BlockSpec((1, capacity, width), lambda i: (1, 0, 0))]
+            * len(pieces),
+            out_specs=pl.BlockSpec((len(pieces), capacity, width), lambda i: (0, 0, 0)),
+            out_shape=shape((len(pieces), capacity, width), bf16),
+            compiler_params=params,
+            cost_estimate=cost(0, 2 << 20),
+        )(*pieces)
+
+    def crossed(a):
+        return lax.ppermute(a, "hi", [(0, 1), (1, 0)])
+
+    blocks = {0: [packed]}
+    behind = ahead = packed
+    near = (0, -1, 1)
     for d in range(1, far):
         behind, ahead = right(behind), left(ahead)
         blocks[-d], blocks[d] = [behind], [ahead]
+        if d == 1:
+            x_near = stacked([blocks[k][0] for k in near])
+            x_near_other = crossed(x_near)
     late = [far - 1, 1 - far, far]
     early = [d for d in blocks if d not in late]
     flat = lambda distances: [b for d in distances for b in blocks[d]]
@@ -308,11 +341,14 @@
         compiler_params=params,
         cost_estimate=cost(2 * macs * len(early), 4 << 20),
     )(order, *flat(early), pre, gate_column)
-    behind, ahead, back, down_early = lax.optimization_barrier(
-        (behind, ahead, back, down_early)
+    behind, ahead, back, down_early, x_near_other = lax.optimization_barrier(
+        (behind, ahead, back, down_early, x_near_other)
     )
     blocks[1 - far], blocks[far - 1] = [behind], [ahead]
-    blocks[far] = [right(behind[:1]), left(ahead[1:])]
+    blocks[far] = [right(behind[:2]), left(ahead[2:])]
+    rest = [d for d in blocks if d not in near]
+    x_rest = stacked([blocks[d][0] for d in rest])
+    x_rest_other = crossed(x_rest)
     pre_grad, gate_mine = pl.pallas_call(
         functools.partial(back_kernel, late, n_rows, True),
         in_specs=[smem] + [vmem] * len(flat(late)) + [hbm, vmem, vmem, vmem],
@@ -340,11 +376,6 @@
         compiler_params=params,
         cost_estimate=cost(2 * macs * 4, 4 << 20),
     )
-    up_early = up_call(
-        functools.partial(up_kernel, early, n_rows, False),
-        in_specs=[smem] + [vmem] * (len(flat(early)) + 1),
-        scratch_shapes=rows_of(len(early) * HI),
-    )(order, *flat(early), pre_grad)
     message = lambda n: shape((n, capacity + EXTRA, width), bf16)
     def begin(d, h):
         return pl.pallas_call(
@@ -377,13 +408,20 @@
         go_right, total_left = carry_on(d, 0 if start else None, from_left, total_left)
         go_left, total_right = carry_on(-d, 1 if start else None, from_right, total_right)
         from_left, from_right = right(go_right), left(go_left)
-    from_left, up_early = lax.optimization_barrier((from_left, up_early))
+    up_early = up_call(
+        functools.partial(up_kernel, near, False),
+        in_specs=[smem, vmem, vmem, vmem],
+        scratch_shapes=rows_of(len(near) * HI),
+    )(order_x, x_near, x_near_other, pre_grad)
+    from_left, up_early, x_rest_other = lax.optimization_barrier(
+        (from_left, up_early, x_rest_other)
+    )
     grad_up = up_call(
-        functools.partial(up_kernel, late, n_rows, True),
-        in_specs=[smem] + [vmem] * (len(flat(late)) + 1) + [hbm],
-        input_output_aliases={len(flat(late)) + 2: 0},
-        scratch_shapes=rows_of(len(late) * HI),
-    )(order, *flat(late), pre_grad, up_early)
+        functools.partial(up_kernel, rest, True),
+        in_specs=[smem, vmem, vmem, vmem, hbm],
+        input_output_aliases={4: 0},
+        scratch_shapes=rows_of(len(rest) * HI),
+    )(order_x, x_rest, x_rest_other, pre_grad, up_early)
     n_gate = capacity // width
     summed, gate_half = pl.pallas_call(
         last_kernel,

time: 169 us -> 162 us (0.959)
  blocking collectives: 32.2 us -> 0 us
  starting transfers between devices: 73.9 us -> 97.5 us
  waiting for transfers between devices: 32.1 us -> 34.1 us
    all_to_all x1 -> x0, blocking collectives: 32.2 us -> none  [per_device(): lax.all_to_all(picked.reshape(HI * n_experts, n_slots, 2 * width), ('hi',...]
    all_to_all x0 -> x1, waiting for transfers between devices: none -> 17.1 us  [per_device(): lax.all_to_all(picked.reshape(HI * n_experts, n_slots, 2 * width), ('hi',...]
    all_to_all x0 -> x1, starting transfers between devices: none -> 14.8 us  [per_device(): lax.all_to_all(picked.reshape(HI * n_experts, n_slots, 2 * width), ('hi',...]
    ppermute x0 -> x2, starting transfers between devices: none -> 11.5 us  [crossed(): return lax.ppermute(a, 'hi', [(0, 1), (1, 0)])]
    ppermute x8, waiting for transfers between devices: 19.6 us -> 9.26 us  [left(): lax.ppermute(a, 'row', [(i, (i - 1) % n_rows) for i in range(n_rows)])]
    ppermute x8, waiting for transfers between devices: 7.81 us -> 3.17 us  [right(): lax.ppermute(a, 'row', [(i, (i + 1) % n_rows) for i in range(n_rows)])]
    all_to_all x1, starting transfers between devices: 14.4 us -> 12.2 us  [per_device(): lax.all_to_all(summed.reshape(HI * n_experts, n_slots, width), ('hi', 'ep...]
    pallas_call x2 -> x5, Pallas kernels: 4.04 us -> 5 us  [the longest x1 2.26 us: per_device(): up_call(functools.partial(up_kernel, near, False), in_specs=[smem, vmem,...]
  transfers between devices with their start and end apart: 18 -> 21, of which waited for: 8 -> 6; matrix products, arithmetic and copies ran while one was open for 0% -> 1% of each run, Pallas kernels for 11% -> 11%
where the time goes in v3:
time: 162 us; the launch traced here: 161 us
  starting transfers between devices  97.5 us (60%)
  waiting for transfers between devices  34.1 us (21%)
  Pallas kernels  25.4 us (16%)
  local copies, waits for them, and re-layouts  2.2 us (1%)
    ppermute x8, starting transfers between devices, left(): lax.ppermute(a, 'row', [(i, (i - 1) % n_rows) for i in range(n_rows)])  38.5 us
    all_to_all x1, waiting for transfers between devices, per_device(): lax.all_to_all(picked.reshape(HI * n_experts, n_slots, 2 * width), ('hi',...  17.1 us
    ppermute x8, starting transfers between devices, right(): lax.ppermute(a, 'row', [(i, (i + 1) % n_rows) for i in range(n_rows)])  15.4 us
    all_to_all x1, starting transfers between devices, per_device(): lax.all_to_all(picked.reshape(HI * n_experts, n_slots, 2 * width), ('hi',...  14.8 us
    all_to_all x1, starting transfers between devices, per_device(): lax.all_to_all(summed.reshape(HI * n_experts, n_slots, width), ('hi', 'ep...  12.2 us
    ppermute x2, starting transfers between devices, crossed(): return lax.ppermute(a, 'hi', [(0, 1), (1, 0)])  11.5 us
    ppermute x8, waiting for transfers between devices, left(): lax.ppermute(a, 'row', [(i, (i - 1) % n_rows) for i in range(n_rows)])  9.26 us
    pallas_call x6, Pallas kernels, carry_on(): pl.pallas_call(functools.partial(pass_kernel, d, only), in_specs=[smem, v...  6.02 us
  transfers between devices with their start and end apart: 21, of which 6 were waited for; matrix products, arithmetic and copies ran while one was open for 1% of the time, Pallas kernels for 11%

profile of v3, /device:TPU:1, one launch (start us, length us, event | category | flops | bytes accessed | tf_op | source)
XLA Modules:
  0.0 161.1 jit_solution(9274081641997477586)
XLA Ops:
  0.6 2.0 %shard_map.111 = (bf16[512,256]{1,0:T(8,128)(2,1)}, bf16[2,512,256]{2,1,0:T(8,128)(2,1)}) custom-call(s32[16,32]{1,0:T(8,128)} %bitcast.34, s32[1,32]{1,0:T(1,128)} %counts_ref.1, bf16[256,128]{1,0:T(8,128)(2,1)} %tokens_ref.1, bf16[256,128]{1,0:T(8,128)(2,1)} %cotangent_ref.1), custom_call_target="tpu_custom_call" | custom-call | tf_op jit(solution)/shard_map/pallas_call | solution.py:274
  2.6 14.8 %all-to-all-start = ((bf16[64,16,256]{2,1,0:T(8,128)(2,1)}), bf16[64,16,256]{2,1,0:T(8,128)(2,1)S(1)}, u32[]{:S(2)}, u32[]{:S(2)}) async-start(bf16[64,16,256]{2,1,0:T(8,128)(2,1)} %bitcast.33), calls=%async_computation | async-start | bytes 1048576 | tf_op jit(solution)/shard_map/all_to_all | solution.py:281
  17.5 0.1 pad_add_fusion.order_ref
  17.6 0.1 pad_add_fusion.1.order_ref
  17.7 17.1 %all-to-all-done = bf16[64,16,256]{2,1,0:T(8,128)(2,1)S(1)} async-done(((bf16[64,16,256]{2,1,0:T(8,128)(2,1)}), bf16[64,16,256]{2,1,0:T(8,128)(2,1)S(1)}, u32[]{:S(2)}, u32[]{:S(2)}) %all-to-all-start) | async-done | bytes 524320 | tf_op jit(solution)/shard_map/all_to_all | solution.py:281
  34.8 0.1 shard_map.112.refs_0_
  34.9 0.0 copy-start.8
  34.9 0.0 copy-start.1
  34.9 5.2 %collective-permute-start.3 = (bf16[3,512,128]{2,1,0:T(8,128)(2,1)S(1)}, bf16[3,512,128]{2,1,0:T(8,128)(2,1)S(1)}, u32[]{:S(2)}, u32[]{:S(2)}) collective-permute-start(bf16[3,512,128]{2,1,0:T(8,128)(2,1)S(1)} %shard_map.112.refs_0_), channel_id=1, source_target_pairs={{0,7},{1,0},{2,1},{3,2},{4,3},{5,4},{6,5},{7,6},{8,15},{9,8},{10,9... | collective-permute-start | bytes 1179656 | tf_op jit(solution)/shard_map/ppermute | solution.py:265
  40.1 1.9 %collective-permute-start = (bf16[3,512,128]{2,1,0:T(8,128)(2,1)S(1)}, bf16[3,512,128]{2,1,0:T(8,128)(2,1)S(1)}, u32[]{:S(2)}, u32[]{:S(2)}) collective-permute-start(bf16[3,512,128]{2,1,0:T(8,128)(2,1)S(1)} %shard_map.112.refs_0_), channel_id=1, source_target_pairs={{0,1},{1,2},{2,3},{3,4},{4,5},{5,6},{6,7},{7,0},{8,9},{9,10},{10,1... | collective-permute-start | bytes 1179656 | tf_op jit(solution)/shard_map/ppermute | solution.py:262
  42.1 6.2 %collective-permute-done.3.refs_2_ = bf16[3,512,128]{2,1,0:T(8,128)(2,1)S(1)} collective-permute-done((bf16[3,512,128]{2,1,0:T(8,128)(2,1)S(1)}, bf16[3,512,128]{2,1,0:T(8,128)(2,1)S(1)}, u32[]{:S(2)}, u32[]{:S(2)}) %collective-permute-start.3) | collective-permute-done | bytes 393248 | tf_op jit(solution)/shard_map/ppermute | solution.py:265
  48.3 5.3 %collective-permute-start.4 = (bf16[3,512,128]{2,1,0:T(8,128)(2,1)S(1)}, bf16[3,512,128]{2,1,0:T(8,128)(2,1)S(1)}, u32[]{:S(2)}, u32[]{:S(2)}) collective-permute-start(bf16[3,512,128]{2,1,0:T(8,128)(2,1)S(1)} %collective-permute-done.3.refs_2_), channel_id=1, source_target_pairs={{0,7},{1,0},{2,1},{3,2},{4,3},{5,4},{6,5},{7,6},{8,15},{9,8},{10,9... | collective-permute-start | bytes 1179656 | tf_op jit(solution)/shard_map/ppermute | solution.py:265
  53.6 0.0 collective-permute-done.refs_1_
  53.6 0.0 copy-start.4
  53.6 1.9 %collective-permute-start.1 = (bf16[3,512,128]{2,1,0:T(8,128)(2,1)S(1)}, bf16[3,512,128]{2,1,0:T(8,128)(2,1)S(1)}, u32[]{:S(2)}, u32[]{:S(2)}) collective-permute-start(bf16[3,512,128]{2,1,0:T(8,128)(2,1)S(1)} %collective-permute-done.refs_1_), channel_id=1, source_target_pairs={{0,1},{1,2},{2,3},{3,4},{4,5},{5,6},{6,7},{7,0},{8,9},{9,10},{10,1... | collective-permute-start | bytes 1179656 | tf_op jit(solution)/shard_map/ppermute | solution.py:262
  55.6 0.8 shard_map.115.own_ref
  56.3 5.2 %collective-permute-start.6 = (bf16[3,512,128]{2,1,0:T(8,128)(2,1)}, bf16[3,512,128]{2,1,0:T(8,128)(2,1)}, u32[]{:S(2)}, u32[]{:S(2)}) collective-permute-start(bf16[3,512,128]{2,1,0:T(8,128)(2,1)} %shard_map.115.own_ref), channel_id=1, source_target_pairs={{0,8},{8,0},{1,9},{9,1},{2,10},{10,2},{3,11},{11,3},{4,12},{12,4},... | collective-permute-start | bytes 1179656 | tf_op jit(solution)/shard_map/ppermute | solution.py:309
  61.6 0.0 collective-permute-done.4.refs_4_.refs_1_
  61.6 4.6 %collective-permute-start.5 = (bf16[3,512,128]{2,1,0:T(8,128)(2,1)S(1)}, bf16[3,512,128]{2,1,0:T(8,128)(2,1)S(1)}, u32[]{:S(2)}, u32[]{:S(2)}) collective-permute-start(bf16[3,512,128]{2,1,0:T(8,128)(2,1)S(1)} %collective-permute-done.4.refs_4_.refs_1_), channel_id=1, source_target_pairs={{0,7},{1,0},{2,1},{3,2},{4,3},{5,4},{6,5},{7,6},{8,15},{9,8},{10,9... | collective-permute-start | bytes 1179656 | tf_op jit(solution)/shard_map/ppermute | solution.py:265
  66.2 0.0 collective-permute-done.1.refs_3_.refs_0_
  66.2 1.9 %collective-permute-start.2 = (bf16[3,512,128]{2,1,0:T(8,128)(2,1)S(1)}, bf16[3,512,128]{2,1,0:T(8,128)(2,1)S(1)}, u32[]{:S(2)}, u32[]{:S(2)}) collective-permute-start(bf16[3,512,128]{2,1,0:T(8,128)(2,1)S(1)} %collective-permute-done.1.refs_3_.refs_0_), channel_id=1, source_target_pairs={{0,1},{1,2},{2,3},{3,4},{4,5},{5,6},{6,7},{7,0},{8,9},{9,10},{10,1... | collective-permute-start | bytes 1179656 | tf_op jit(solution)/shard_map/ppermute | solution.py:262
  68.1 0.1 copy.14.refs_6_.refs_7_.refs_5_
  68.3 0.0 copy-start.3
  68.3 1.0 copy-done.3
  69.3 1.0 copy-done.5
  70.3 2.0 %shard_map.113.refs_5_ = f32[512,256]{1,0:T(8,128)S(1)} custom-call(s32[16]{0:T(128)S(1)} %pad_add_fusion.order_ref, bf16[3,512,128]{2,1,0:T(8,128)(2,1)S(1)} %shard_map.112.refs_0_, bf16[3,512,128]{2,1,0:T(8,128)(2,1)S(1)} %copy-done.5, bf16[3,512,128]{2,1,0:T(8,128)(2,1)S(1)} %copy-done.3, bf16[3,512,128]{2,1,0:T(8,128)(2,1)S(1)} %collective-permute-done.1.refs_3_.refs_0_, ...), custom_call_target="tpu_custom_call" | custom-call | flops 335544320 | bytes 4194304 | tf_op jit(solution)/shard_map/pallas_call | solution.py:326
  72.3 2.0 %shard_map.114.refs_6_ = bf16[256,2048]{1,0:T(8,128)(2,1)} custom-call(s32[16]{0:T(128)S(1)} %pad_add_fusion.order_ref, bf16[3,512,128]{2,1,0:T(8,128)(2,1)S(1)} %shard_map.112.refs_0_, bf16[3,512,128]{2,1,0:T(8,128)(2,1)S(1)} %copy-done.5, bf16[3,512,128]{2,1,0:T(8,128)(2,1)S(1)} %copy-done.3, ...), custom_call_target="tpu_custom_call" | custom-call | flops 335544320 | bytes 4194304 | tf_op jit(solution)/shard_map/pallas_call | solution.py:335
  74.4 0.0 collective-permute-done.6.other_ref
  74.4 0.0 collective-permute-done.5.refs_0_.refs_3_
  74.4 3.2 %collective-permute-done.2.refs_1_.refs_2_ = bf16[3,512,128]{2,1,0:T(8,128)(2,1)S(1)} collective-permute-done((bf16[3,512,128]{2,1,0:T(8,128)(2,1)S(1)}, bf16[3,512,128]{2,1,0:T(8,128)(2,1)S(1)}, u32[]{:S(2)}, u32[]{:S(2)}) %collective-permute-start.2) | collective-permute-done | bytes 393248 | tf_op jit(solution)/shard_map/ppermute | solution.py:262
  77.6 1.9 %collective-permute-start.7 = (bf16[2,512,128]{2,1,0:T(8,128)(2,1)S(1)}, bf16[2,512,128]{2,1,0:T(8,128)(2,1)S(1)}, u32[]{:S(2)}, u32[]{:S(2)}) collective-permute-start(bf16[2,512,128]{2,1,0:T(8,128)(2,1)S(1)} %slice.6), channel_id=1, source_target_pairs={{0,1},{1,2},{2,3},{3,4},{4,5},{5,6},{6,7},{7,0},{8,9},{9,10},{10,1... | collective-permute-start | bytes 786440 | tf_op jit(solution)/shard_map/ppermute | solution.py:262
  79.5 0.0 copy-start
  79.5 4.7 %collective-permute-start.8 = (bf16[1,512,128]{2,1,0:T(8,128)(2,1)S(1)}, bf16[1,512,128]{2,1,0:T(8,128)(2,1)S(1)}, u32[]{:S(2)}, u32[]{:S(2)}) collective-permute-start(bf16[1,512,128]{2,1,0:T(8,128)(2,1)S(1)} %slice.7), channel_id=1, source_target_pairs={{0,7},{1,0},{2,1},{3,2},{4,3},{5,4},{6,5},{7,6},{8,15},{9,8},{10,9... | collective-permute-start | bytes 393224 | tf_op jit(solution)/shard_map/ppermute | solution.py:265
  84.2 1.9 %collective-permute-done.8.refs_3_ = bf16[1,512,128]{2,1,0:T(8,128)(2,1)S(1)} collective-permute-done((bf16[1,512,128]{2,1,0:T(8,128)(2,1)S(1)}, bf16[1,512,128]{2,1,0:T(8,128)(2,1)S(1)}, u32[]{:S(2)}, u32[]{:S(2)}) %collective-permute-start.8) | collective-permute-done | bytes 131104 | tf_op jit(solution)/shard_map/ppermute | solution.py:265
  86.2 0.0 collective-permute-done.7.refs_2_.refs_4_
  86.2 2.1 %shard_map.116 = (bf16[512,256]{1,0:T(8,128)(2,1)S(1)}, f32[16,128]{1,0:T(8,128)S(1)}) custom-call(s32[16]{0:T(128)S(1)} %pad_add_fusion.order_ref, bf16[3,512,128]{2,1,0:T(8,128)(2,1)S(1)} %collective-permute-done.5.refs_0_.refs_3_, bf16[3,512,128]{2,1,0:T(8,128)(2,1)S(1)} %collective-permute-done.2.refs_1_.refs_2_, ...), custom_call_target="tpu_custom_call" | custom-call | flops 201326592 | bytes 3145728 | tf_op jit(solution)/shard_map/pallas_call | solution.py:352
  88.3 0.9 shard_map.117
  89.2 1.9 %collective-permute-start.9 = (bf16[1,528,128]{2,1,0:T(8,128)(2,1)S(1)}, bf16[1,528,128]{2,1,0:T(8,128)(2,1)S(1)}, u32[]{:S(2)}, u32[]{:S(2)}) collective-permute-start(bf16[1,528,128]{2,1,0:T(8,128)(2,1)S(1)} %shard_map.117), channel_id=1, source_target_pairs={{0,1},{1,2},{2,3},{3,4},{4,5},{5,6},{6,7},{7,0},{8,9},{9,10},{10,1... | collective-permute-start | bytes 405512 | tf_op jit(solution)/shard_map/ppermute | solution.py:262
  91.1 0.9 shard_map.124
  92.0 5.0 %collective-permute-start.14 = (bf16[1,528,128]{2,1,0:T(8,128)(2,1)S(1)}, bf16[1,528,128]{2,1,0:T(8,128)(2,1)S(1)}, u32[]{:S(2)}, u32[]{:S(2)}) collective-permute-start(bf16[1,528,128]{2,1,0:T(8,128)(2,1)S(1)} %shard_map.124), channel_id=1, source_target_pairs={{0,7},{1,0},{2,1},{3,2},{4,3},{5,4},{6,5},{7,6},{8,15},{9,8},{10,9... | collective-permute-start | bytes 405512 | tf_op jit(solution)/shard_map/ppermute | solution.py:265
  97.0 0.0 collective-permute-done.9.came
  97.0 1.0 shard_map.118
  98.0 1.9 %collective-permute-start.10 = (bf16[2,528,128]{2,1,0:T(8,128)(2,1)S(1)}, bf16[2,528,128]{2,1,0:T(8,128)(2,1)S(1)}, u32[]{:S(2)}, u32[]{:S(2)}) collective-permute-start(bf16[2,528,128]{2,1,0:T(8,128)(2,1)S(1)} %get-tuple-element.46), channel_id=1, source_target_pairs={{0,1},{1,2},{2,3},{3,4},{4,5},{5,6},{6,7},{7,0},{8,9},{9,10},{10,1... | collective-permute-start | bytes 811016 | tf_op jit(solution)/shard_map/ppermute | solution.py:262
  100.0 1.0 shard_map.125
  101.0 4.6 %collective-permute-start.15 = (bf16[2,528,128]{2,1,0:T(8,128)(2,1)S(1)}, bf16[2,528,128]{2,1,0:T(8,128)(2,1)S(1)}, u32[]{:S(2)}, u32[]{:S(2)}) collective-permute-start(bf16[2,528,128]{2,1,0:T(8,128)(2,1)S(1)} %get-tuple-element.56), channel_id=1, source_target_pairs={{0,7},{1,0},{2,1},{3,2},{4,3},{5,4},{6,5},{7,6},{8,15},{9,8},{10,9... | collective-permute-start | bytes 811016 | tf_op jit(solution)/shard_map/ppermute | solution.py:265
  105.6 6.3 %collective-permute-start.13 = (bf16[5,512,128]{2,1,0:T(8,128)(2,1)S(1)}, bf16[5,512,128]{2,1,0:T(8,128)(2,1)S(1)}, u32[]{:S(2)}, u32[]{:S(2)}) collective-permute-start(bf16[5,512,128]{2,1,0:T(8,128)(2,1)S(1)} %shard_map.123.own_ref), channel_id=1, source_target_pairs={{0,8},{8,0},{1,9},{9,1},{2,10},{10,2},{3,11},{11,3},{4,12},{12,4},... | collective-permute-start | bytes 1966088 | tf_op jit(solution)/shard_map/ppermute | solution.py:309
  111.9 1.0 shard_map.119
  112.9 1.9 %collective-permute-start.11 = (bf16[2,528,128]{2,1,0:T(8,128)(2,1)S(1)}, bf16[2,528,128]{2,1,0:T(8,128)(2,1)S(1)}, u32[]{:S(2)}, u32[]{:S(2)}) collective-permute-start(bf16[2,528,128]{2,1,0:T(8,128)(2,1)S(1)} %get-tuple-element.48), channel_id=1, source_target_pairs={{0,1},{1,2},{2,3},{3,4},{4,5},{5,6},{6,7},{7,0},{8,9},{9,10},{10,1... | collective-permute-start | bytes 811016 | tf_op jit(solution)/shard_map/ppermute | solution.py:262
  114.9 1.0 shard_map.126
  115.9 4.6 %collective-permute-start.16 = (bf16[2,528,128]{2,1,0:T(8,128)(2,1)S(1)}, bf16[2,528,128]{2,1,0:T(8,128)(2,1)S(1)}, u32[]{:S(2)}, u32[]{:S(2)}) collective-permute-start(bf16[2,528,128]{2,1,0:T(8,128)(2,1)S(1)} %get-tuple-element.58), channel_id=1, source_target_pairs={{0,7},{1,0},{2,1},{3,2},{4,3},{5,4},{6,5},{7,6},{8,15},{9,8},{10,9... | collective-permute-start | bytes 811016 | tf_op jit(solution)/shard_map/ppermute | solution.py:265
  120.5 1.9 %shard_map.120 = bf16[256,2048]{1,0:T(8,128)(2,1)} custom-call(s32[16]{0:T(128)S(1)} %pad_add_fusion.order_ref, bf16[3,512,128]{2,1,0:T(8,128)(2,1)S(1)} %collective-permute-done.5.refs_0_.refs_3_, bf16[3,512,128]{2,1,0:T(8,128)(2,1)S(1)} %collective-permute-done.2.refs_1_.refs_2_, ...), custom_call_target="tpu_custom_call", output_to_operand_aliasing={{}: (7, {})} | custom-call | flops 201326592 | bytes 3145728 | tf_op jit(solution)/shard_map/pallas_call | solution.py:362
  122.3 1.0 shard_map.121
  123.3 1.9 %collective-permute-start.12 = (bf16[2,528,128]{2,1,0:T(8,128)(2,1)S(1)}, bf16[2,528,128]{2,1,0:T(8,128)(2,1)S(1)}, u32[]{:S(2)}, u32[]{:S(2)}) collective-permute-start(bf16[2,528,128]{2,1,0:T(8,128)(2,1)S(1)} %get-tuple-element.52), channel_id=1, source_target_pairs={{0,1},{1,2},{2,3},{3,4},{4,5},{5,6},{6,7},{7,0},{8,9},{9,10},{10,1... | collective-permute-start | bytes 811016 | tf_op jit(solution)/shard_map/ppermute | solution.py:262
  125.3 1.0 shard_map.127
  126.3 4.6 %collective-permute-start.17 = (bf16[2,528,128]{2,1,0:T(8,128)(2,1)S(1)}, bf16[2,528,128]{2,1,0:T(8,128)(2,1)S(1)}, u32[]{:S(2)}, u32[]{:S(2)}) collective-permute-start(bf16[2,528,128]{2,1,0:T(8,128)(2,1)S(1)} %get-tuple-element.60), channel_id=1, source_target_pairs={{0,7},{1,0},{2,1},{3,2},{4,3},{5,4},{6,5},{7,6},{8,15},{9,8},{10,9... | collective-permute-start | bytes 811016 | tf_op jit(solution)/shard_map/ppermute | solution.py:265
  130.9 2.3 %shard_map.122.refs_0_ = bf16[2048,256]{1,0:T(8,128)(2,1)} custom-call(s32[16]{0:T(128)S(1)} %pad_add_fusion.1.order_ref, bf16[3,512,128]{2,1,0:T(8,128)(2,1)} %shard_map.115.own_ref, bf16[3,512,128]{2,1,0:T(8,128)(2,1)} %collective-permute-done.6.other_ref, bf16[512,256]{1,0:T(8,128)(2,1)S(1)} %get-tuple-element.44.pre_grad_ref), custom_call_target="tpu_custom_call" | custom-call | flops 268435456 | bytes 4194304 | tf_op jit(solution)/shard_map/pallas_call | solution.py:411
  133.2 1.1 collective-permute-done.17.from_right
  134.3 1.7 %shard_map.128 = (bf16[2,512,128]{2,1,0:T(8,128)(2,1)}, f32[4,128]{1,0:T(4,128)S(1)}) custom-call(s32[16]{0:T(128)S(1)} %pad_add_fusion.order_ref, bf16[2,528,128]{2,1,0:T(8,128)(2,1)S(1)} %collective-permute-done.12.from_left, bf16[2,528,128]{2,1,0:T(8,128)(2,1)S(1)} %collective-permute-done.17.from_right, ...), custom_call_target="tpu_custom_call" | custom-call | flops 67108864 | bytes 2097152 | tf_op jit(solution)/shard_map/pallas_call | solution.py:426
  136.0 12.2 %all-to-all-start.1 = ((bf16[64,16,128]{2,1,0:T(8,128)(2,1)}), bf16[64,16,128]{2,1,0:T(8,128)(2,1)S(1)}, u32[]{:S(2)}, u32[]{:S(2)}) async-start(bf16[64,16,128]{2,1,0:T(8,128)(2,1)} %bitcast.9), calls=%async_computation.1 | async-start | bytes 524288 | tf_op jit(solution)/shard_map/all_to_all | solution.py:436
  148.2 5.0 %collective-permute-start.18 = (f32[4,128]{1,0:T(4,128)S(1)}, f32[4,128]{1,0:T(4,128)S(1)}, u32[]{:S(2)}, u32[]{:S(2)}) collective-permute-start(f32[4,128]{1,0:T(4,128)S(1)} %get-tuple-element.67), channel_id=1, source_target_pairs={{0,8},{8,0},{1,9},{9,1},{2,10},{10,2},{3,11},{11,3},{4,12},{12,4},... | collective-permute-start | bytes 6152 | tf_op jit(solution)/shard_map/ppermute | solution.py:435
  153.3 1.9 %shard_map.130 = bf16[2048,256]{1,0:T(8,128)(2,1)} custom-call(s32[16]{0:T(128)S(1)} %pad_add_fusion.1.order_ref, bf16[5,512,128]{2,1,0:T(8,128)(2,1)S(1)} %shard_map.123.own_ref, bf16[5,512,128]{2,1,0:T(8,128)(2,1)S(1)} %collective-permute-done.13.other_ref, bf16[512,256]{1,0:T(8,128)(2,1)S(1)} %get-tuple-element.44.pre_grad_ref, ...), custom_call_target="tpu_custom_call", output_to_operand_aliasing={{}: (4, {})} | custom-call | flops 268435456 | bytes 4194304 | tf_op jit(solution)/shard_map/pallas_call | solution.py:419
  155.1 0.6 add.38
  155.7 4.5 %all-to-all-done.1 = bf16[64,16,128]{2,1,0:T(8,128)(2,1)S(1)} async-done(((bf16[64,16,128]{2,1,0:T(8,128)(2,1)}), bf16[64,16,128]{2,1,0:T(8,128)(2,1)S(1)}, u32[]{:S(2)}, u32[]{:S(2)}) %all-to-all-start.1) | async-done | bytes 262176 | tf_op jit(solution)/shard_map/all_to_all | solution.py:436
  160.2 0.9 shard_map.129
  (25 shorter events, 0.1 us)
Async XLA Ops:
  2.6 32.2 %all-to-all-start = ((bf16[64,16,256]{2,1,0:T(8,128)(2,1)}), bf16[64,16,256]{2,1,0:T(8,128)(2,1)S(1)}, u32[]{:S(2)}, u32[]{:S(2)}) async-start(bf16[64,16,256]{2,1,0:T(8,128)(2,1)} %bitcast.33), calls=%async_computation | async-start | bytes 1048576 | tf_op jit(solution)/shard_map/all_to_all | solution.py:281
  34.9 33.2 %copy-start.8 = (f32[1,512]{1,0:T(1,128)S(1)}, f32[1,512]{1,0:T(1,128)}, u32[]{:S(2)}) copy-start(f32[1,512]{1,0:T(1,128)} %param.13) | copy-start | bytes 6148
  34.9 33.4 %copy-start.1 = (bf16[1,256,2048]{2,1,0:T(8,128)(2,1)S(1)}, bf16[1,256,2048]{2,1,0:T(8,128)(2,1)}, u32[]{:S(2)}) copy-start(bf16[1,256,2048]{2,1,0:T(8,128)(2,1)} %param.11) | copy-start | bytes 3145732
  34.9 13.4 %collective-permute-start.3 = (bf16[3,512,128]{2,1,0:T(8,128)(2,1)S(1)}, bf16[3,512,128]{2,1,0:T(8,128)(2,1)S(1)}, u32[]{:S(2)}, u32[]{:S(2)}) collective-permute-start(bf16[3,512,128]{2,1,0:T(8,128)(2,1)S(1)} %shard_map.112.refs_0_), channel_id=1, source_target_pairs={{0,7},{1,0},{2,1},{3,2},{4,3},{5,4},{6,5},{7,6},{8,15},{9,8},{10,9... | collective-permute-start | bytes 1179656 | tf_op jit(solution)/shard_map/ppermute | solution.py:265
  40.1 13.5 %collective-permute-start = (bf16[3,512,128]{2,1,0:T(8,128)(2,1)S(1)}, bf16[3,512,128]{2,1,0:T(8,128)(2,1)S(1)}, u32[]{:S(2)}, u32[]{:S(2)}) collective-permute-start(bf16[3,512,128]{2,1,0:T(8,128)(2,1)S(1)} %shard_map.112.refs_0_), channel_id=1, source_target_pairs={{0,1},{1,2},{2,3},{3,4},{4,5},{5,6},{6,7},{7,0},{8,9},{9,10},{10,1... | collective-permute-start | bytes 1179656 | tf_op jit(solution)/shard_map/ppermute | solution.py:262
  48.3 8.0 %copy-start.2 = (bf16[3,512,128]{2,1,0:T(8,128)(2,1)}, bf16[3,512,128]{2,1,0:T(8,128)(2,1)S(1)}, u32[]{:S(2)}) copy-start(bf16[3,512,128]{2,1,0:T(8,128)(2,1)S(1)} %collective-permute-done.3.refs_2_) | copy-start | bytes 1179652
  48.3 13.3 %collective-permute-start.4 = (bf16[3,512,128]{2,1,0:T(8,128)(2,1)S(1)}, bf16[3,512,128]{2,1,0:T(8,128)(2,1)S(1)}, u32[]{:S(2)}, u32[]{:S(2)}) collective-permute-start(bf16[3,512,128]{2,1,0:T(8,128)(2,1)S(1)} %collective-permute-done.3.refs_2_), channel_id=1, source_target_pairs={{0,7},{1,0},{2,1},{3,2},{4,3},{5,4},{6,5},{7,6},{8,15},{9,8},{10,9... | collective-permute-start | bytes 1179656 | tf_op jit(solution)/shard_map/ppermute | solution.py:265
  53.6 2.7 %copy-start.4 = (bf16[3,512,128]{2,1,0:T(8,128)(2,1)}, bf16[3,512,128]{2,1,0:T(8,128)(2,1)S(1)}, u32[]{:S(2)}) copy-start(bf16[3,512,128]{2,1,0:T(8,128)(2,1)S(1)} %collective-permute-done.refs_1_) | copy-start | bytes 1179652
  53.6 12.5 %collective-permute-start.1 = (bf16[3,512,128]{2,1,0:T(8,128)(2,1)S(1)}, bf16[3,512,128]{2,1,0:T(8,128)(2,1)S(1)}, u32[]{:S(2)}, u32[]{:S(2)}) collective-permute-start(bf16[3,512,128]{2,1,0:T(8,128)(2,1)S(1)} %collective-permute-done.refs_1_), channel_id=1, source_target_pairs={{0,1},{1,2},{2,3},{3,4},{4,5},{5,6},{6,7},{7,0},{8,9},{9,10},{10,1... | collective-permute-start | bytes 1179656 | tf_op jit(solution)/shard_map/ppermute | solution.py:262
  56.3 18.0 %collective-permute-start.6 = (bf16[3,512,128]{2,1,0:T(8,128)(2,1)}, bf16[3,512,128]{2,1,0:T(8,128)(2,1)}, u32[]{:S(2)}, u32[]{:S(2)}) collective-permute-start(bf16[3,512,128]{2,1,0:T(8,128)(2,1)} %shard_map.115.own_ref), channel_id=1, source_target_pairs={{0,8},{8,0},{1,9},{9,1},{2,10},{10,2},{3,11},{11,3},{4,12},{12,4},... | collective-permute-start | bytes 1179656 | tf_op jit(solution)/shard_map/ppermute | solution.py:309
  61.6 12.8 %collective-permute-start.5 = (bf16[3,512,128]{2,1,0:T(8,128)(2,1)S(1)}, bf16[3,512,128]{2,1,0:T(8,128)(2,1)S(1)}, u32[]{:S(2)}, u32[]{:S(2)}) collective-permute-start(bf16[3,512,128]{2,1,0:T(8,128)(2,1)S(1)} %collective-permute-done.4.refs_4_.refs_1_), channel_id=1, source_target_pairs={{0,7},{1,0},{2,1},{3,2},{4,3},{5,4},{6,5},{7,6},{8,15},{9,8},{10,9... | collective-permute-start | bytes 1179656 | tf_op jit(solution)/shard_map/ppermute | solution.py:265
  66.2 11.4 %collective-permute-start.2 = (bf16[3,512,128]{2,1,0:T(8,128)(2,1)S(1)}, bf16[3,512,128]{2,1,0:T(8,128)(2,1)S(1)}, u32[]{:S(2)}, u32[]{:S(2)}) collective-permute-start(bf16[3,512,128]{2,1,0:T(8,128)(2,1)S(1)} %collective-permute-done.1.refs_3_.refs_0_), channel_id=1, source_target_pairs={{0,1},{1,2},{2,3},{3,4},{4,5},{5,6},{6,7},{7,0},{8,9},{9,10},{10,1... | collective-permute-start | bytes 1179656 | tf_op jit(solution)/shard_map/ppermute | solution.py:262
  68.3 1.0 copy-start.3
  69.3 1.0 copy-start.5
  70.3 2.0 %copy-start.6 = (bf16[1,512,256]{2,1,0:T(8,128)(2,1)S(1)}, bf16[1,512,256]{2,1,0:T(8,128)(2,1)}, u32[]{:S(2)}) copy-start(bf16[1,512,256]{2,1,0:T(8,128)(2,1)} %param.12) | copy-start | bytes 786436
  77.6 8.6 %collective-permute-start.7 = (bf16[2,512,128]{2,1,0:T(8,128)(2,1)S(1)}, bf16[2,512,128]{2,1,0:T(8,128)(2,1)S(1)}, u32[]{:S(2)}, u32[]{:S(2)}) collective-permute-start(bf16[2,512,128]{2,1,0:T(8,128)(2,1)S(1)} %slice.6), channel_id=1, source_target_pairs={{0,1},{1,2},{2,3},{3,4},{4,5},{5,6},{6,7},{7,0},{8,9},{9,10},{10,1... | collective-permute-start | bytes 786440 | tf_op jit(solution)/shard_map/ppermute | solution.py:262
  79.5 8.8 %copy-start = (bf16[1,2048,256]{2,1,0:T(8,128)(2,1)S(1)}, bf16[1,2048,256]{2,1,0:T(8,128)(2,1)}, u32[]{:S(2)}) copy-start(bf16[1,2048,256]{2,1,0:T(8,128)(2,1)} %param.10) | copy-start | bytes 3145732
  79.5 6.6 %collective-permute-start.8 = (bf16[1,512,128]{2,1,0:T(8,128)(2,1)S(1)}, bf16[1,512,128]{2,1,0:T(8,128)(2,1)S(1)}, u32[]{:S(2)}, u32[]{:S(2)}) collective-permute-start(bf16[1,512,128]{2,1,0:T(8,128)(2,1)S(1)} %slice.7), channel_id=1, source_target_pairs={{0,7},{1,0},{2,1},{3,2},{4,3},{5,4},{6,5},{7,6},{8,15},{9,8},{10,9... | collective-permute-start | bytes 393224 | tf_op jit(solution)/shard_map/ppermute | solution.py:265
  89.2 7.8 %collective-permute-start.9 = (bf16[1,528,128]{2,1,0:T(8,128)(2,1)S(1)}, bf16[1,528,128]{2,1,0:T(8,128)(2,1)S(1)}, u32[]{:S(2)}, u32[]{:S(2)}) collective-permute-start(bf16[1,528,128]{2,1,0:T(8,128)(2,1)S(1)} %shard_map.117), channel_id=1, source_target_pairs={{0,1},{1,2},{2,3},{3,4},{4,5},{5,6},{6,7},{7,0},{8,9},{9,10},{10,1... | collective-permute-start | bytes 405512 | tf_op jit(solution)/shard_map/ppermute | solution.py:262
  92.0 8.0 %collective-permute-start.14 = (bf16[1,528,128]{2,1,0:T(8,128)(2,1)S(1)}, bf16[1,528,128]{2,1,0:T(8,128)(2,1)S(1)}, u32[]{:S(2)}, u32[]{:S(2)}) collective-permute-start(bf16[1,528,128]{2,1,0:T(8,128)(2,1)S(1)} %shard_map.124), channel_id=1, source_target_pairs={{0,7},{1,0},{2,1},{3,2},{4,3},{5,4},{6,5},{7,6},{8,15},{9,8},{10,9... | collective-permute-start | bytes 405512 | tf_op jit(solution)/shard_map/ppermute | solution.py:265
  98.0 13.9 %collective-permute-start.10 = (bf16[2,528,128]{2,1,0:T(8,128)(2,1)S(1)}, bf16[2,528,128]{2,1,0:T(8,128)(2,1)S(1)}, u32[]{:S(2)}, u32[]{:S(2)}) collective-permute-start(bf16[2,528,128]{2,1,0:T(8,128)(2,1)S(1)} %get-tuple-element.46), channel_id=1, source_target_pairs={{0,1},{1,2},{2,3},{3,4},{4,5},{5,6},{6,7},{7,0},{8,9},{9,10},{10,1... | collective-permute-start | bytes 811016 | tf_op jit(solution)/shard_map/ppermute | solution.py:262
  101.0 13.9 %collective-permute-start.15 = (bf16[2,528,128]{2,1,0:T(8,128)(2,1)S(1)}, bf16[2,528,128]{2,1,0:T(8,128)(2,1)S(1)}, u32[]{:S(2)}, u32[]{:S(2)}) collective-permute-start(bf16[2,528,128]{2,1,0:T(8,128)(2,1)S(1)} %get-tuple-element.56), channel_id=1, source_target_pairs={{0,7},{1,0},{2,1},{3,2},{4,3},{5,4},{6,5},{7,6},{8,15},{9,8},{10,9... | collective-permute-start | bytes 811016 | tf_op jit(solution)/shard_map/ppermute | solution.py:265
  105.6 27.5 %collective-permute-start.13 = (bf16[5,512,128]{2,1,0:T(8,128)(2,1)S(1)}, bf16[5,512,128]{2,1,0:T(8,128)(2,1)S(1)}, u32[]{:S(2)}, u32[]{:S(2)}) collective-permute-start(bf16[5,512,128]{2,1,0:T(8,128)(2,1)S(1)} %shard_map.123.own_ref), channel_id=1, source_target_pairs={{0,8},{8,0},{1,9},{9,1},{2,10},{10,2},{3,11},{11,3},{4,12},{12,4},... | collective-permute-start | bytes 1966088 | tf_op jit(solution)/shard_map/ppermute | solution.py:309
  112.9 9.4 %collective-permute-start.11 = (bf16[2,528,128]{2,1,0:T(8,128)(2,1)S(1)}, bf16[2,528,128]{2,1,0:T(8,128)(2,1)S(1)}, u32[]{:S(2)}, u32[]{:S(2)}) collective-permute-start(bf16[2,528,128]{2,1,0:T(8,128)(2,1)S(1)} %get-tuple-element.48), channel_id=1, source_target_pairs={{0,1},{1,2},{2,3},{3,4},{4,5},{5,6},{6,7},{7,0},{8,9},{9,10},{10,1... | collective-permute-start | bytes 811016 | tf_op jit(solution)/shard_map/ppermute | solution.py:262
  115.9 9.4 %collective-permute-start.16 = (bf16[2,528,128]{2,1,0:T(8,128)(2,1)S(1)}, bf16[2,528,128]{2,1,0:T(8,128)(2,1)S(1)}, u32[]{:S(2)}, u32[]{:S(2)}) collective-permute-start(bf16[2,528,128]{2,1,0:T(8,128)(2,1)S(1)} %get-tuple-element.58), channel_id=1, source_target_pairs={{0,7},{1,0},{2,1},{3,2},{4,3},{5,4},{6,5},{7,6},{8,15},{9,8},{10,9... | collective-permute-start | bytes 811016 | tf_op jit(solution)/shard_map/ppermute | solution.py:265
  123.3 9.8 %collective-permute-start.12 = (bf16[2,528,128]{2,1,0:T(8,128)(2,1)S(1)}, bf16[2,528,128]{2,1,0:T(8,128)(2,1)S(1)}, u32[]{:S(2)}, u32[]{:S(2)}) collective-permute-start(bf16[2,528,128]{2,1,0:T(8,128)(2,1)S(1)} %get-tuple-element.52), channel_id=1, source_target_pairs={{0,1},{1,2},{2,3},{3,4},{4,5},{5,6},{6,7},{7,0},{8,9},{9,10},{10,1... | collective-permute-start | bytes 811016 | tf_op jit(solution)/shard_map/ppermute | solution.py:262
  126.3 8.0 %collective-permute-start.17 = (bf16[2,528,128]{2,1,0:T(8,128)(2,1)S(1)}, bf16[2,528,128]{2,1,0:T(8,128)(2,1)S(1)}, u32[]{:S(2)}, u32[]{:S(2)}) collective-permute-start(bf16[2,528,128]{2,1,0:T(8,128)(2,1)S(1)} %get-tuple-element.60), channel_id=1, source_target_pairs={{0,7},{1,0},{2,1},{3,2},{4,3},{5,4},{6,5},{7,6},{8,15},{9,8},{10,9... | collective-permute-start | bytes 811016 | tf_op jit(solution)/shard_map/ppermute | solution.py:265
  136.0 24.2 %all-to-all-start.1 = ((bf16[64,16,128]{2,1,0:T(8,128)(2,1)}), bf16[64,16,128]{2,1,0:T(8,128)(2,1)S(1)}, u32[]{:S(2)}, u32[]{:S(2)}) async-start(bf16[64,16,128]{2,1,0:T(8,128)(2,1)} %bitcast.9), calls=%async_computation.1 | async-start | bytes 524288 | tf_op jit(solution)/shard_map/all_to_all | solution.py:436
  148.2 12.0 %copy-start.7 = (bf16[512,256]{1,0:T(8,128)(2,1)S(1)}, bf16[512,256]{1,0:T(8,128)(2,1)}, u32[]{:S(2)}) copy-start(bf16[512,256]{1,0:T(8,128)(2,1)} %get-tuple-element.36.sel_ref) | copy-start | bytes 786436
  148.2 6.9 %collective-permute-start.18 = (f32[4,128]{1,0:T(4,128)S(1)}, f32[4,128]{1,0:T(4,128)S(1)}, u32[]{:S(2)}, u32[]{:S(2)}) collective-permute-start(f32[4,128]{1,0:T(4,128)S(1)} %get-tuple-element.67), channel_id=1, source_target_pairs={{0,8},{8,0},{1,9},{9,1},{2,10},{10,2},{3,11},{11,3},{4,12},{12,4},... | collective-permute-start | bytes 6152 | tf_op jit(solution)/shard_map/ppermute | solution.py:435

commit v4 on v3

--- a/solution.py
+++ b/solution.py
@@ -310,14 +310,14 @@
 
     blocks = {0: [packed]}
     behind = ahead = packed
-    near = (0, -1, 1)
+    near = (0, 1, -1)
     for d in range(1, far):
-        behind, ahead = right(behind), left(ahead)
-        blocks[-d], blocks[d] = [behind], [ahead]
+        ahead, behind = left(ahead), right(behind)
+        blocks[d], blocks[-d] = [ahead], [behind]
         if d == 1:
             x_near = stacked([blocks[k][0] for k in near])
             x_near_other = crossed(x_near)
-    late = [far - 1, 1 - far, far]
+    late = [1 - far, far - 1, far]
     early = [d for d in blocks if d not in late]
     flat = lambda distances: [b for d in distances for b in blocks[d]]
     columns = lambda n: [pltpu.VMEM((units, n * HI * width), bf16), dma((n * HI,))]
@@ -341,8 +341,8 @@
         compiler_params=params,
         cost_estimate=cost(2 * macs * len(early), 4 << 20),
     )(order, *flat(early), pre, gate_column)
-    behind, ahead, back, down_early, x_near_other = lax.optimization_barrier(
-        (behind, ahead, back, down_early, x_near_other)
+    ahead, behind, back, down_early, x_near_other = lax.optimization_barrier(
+        (ahead, behind, back, down_early, x_near_other)
     )
     blocks[1 - far], blocks[far - 1] = [behind], [ahead]
     blocks[far] = [right(behind[:2]), left(ahead[2:])]

time: 162 us -> 161 us (level)
    ppermute x8, starting transfers between devices: 38.5 us -> 32.4 us  [left(): lax.ppermute(a, 'row', [(i, (i - 1) % n_rows) for i in range(n_rows)])]
    ppermute x8, starting transfers between devices: 15.4 us -> 21 us  [right(): lax.ppermute(a, 'row', [(i, (i + 1) % n_rows) for i in range(n_rows)])]
    ppermute x8, waiting for transfers between devices: 9.26 us -> 3.63 us  [left(): lax.ppermute(a, 'row', [(i, (i - 1) % n_rows) for i in range(n_rows)])]
    ppermute x8, waiting for transfers between devices: 3.17 us -> 7.82 us  [right(): lax.ppermute(a, 'row', [(i, (i + 1) % n_rows) for i in range(n_rows)])]
  transfers between devices with their start and end apart: 21 -> 21, of which waited for: 6 -> 7; matrix products, arithmetic and copies ran while one was open for 1% -> 1% of each run, Pallas kernels for 11% -> 11%
where the time goes in v4:
time: 161 us; the launch traced here: 159 us
  starting transfers between devices  96.4 us (60%)
  waiting for transfers between devices  33.1 us (21%)
  Pallas kernels  25.4 us (16%)
  local copies, waits for them, and re-layouts  2.2 us (1%)
    ppermute x8, starting transfers between devices, left(): lax.ppermute(a, 'row', [(i, (i - 1) % n_rows) for i in range(n_rows)])  32.4 us
    ppermute x8, starting transfers between devices, right(): lax.ppermute(a, 'row', [(i, (i + 1) % n_rows) for i in range(n_rows)])  21 us
    all_to_all x1, waiting for transfers between devices, per_device(): lax.all_to_all(picked.reshape(HI * n_experts, n_slots, 2 * width), ('hi',...  17.1 us
    all_to_all x1, starting transfers between devices, per_device(): lax.all_to_all(picked.reshape(HI * n_experts, n_slots, 2 * width), ('hi',...  14.8 us
    all_to_all x1, starting transfers between devices, per_device(): lax.all_to_all(summed.reshape(HI * n_experts, n_slots, width), ('hi', 'ep...  11.7 us
    ppermute x2, starting transfers between devices, crossed(): return lax.ppermute(a, 'hi', [(0, 1), (1, 0)])  11.4 us
    ppermute x8, waiting for transfers between devices, right(): lax.ppermute(a, 'row', [(i, (i + 1) % n_rows) for i in range(n_rows)])  7.82 us
    pallas_call x6, Pallas kernels, carry_on(): pl.pallas_call(functools.partial(pass_kernel, d, only), in_specs=[smem, v...  6.02 us
  transfers between devices with their start and end apart: 21, of which 7 were waited for; matrix products, arithmetic and copies ran while one was open for 1% of the time, Pallas kernels for 11%

profile of v4, /device:TPU:1, one launch (start us, length us, event | category | flops | bytes accessed | tf_op | source)
XLA Modules:
  0.0 159.0 jit_solution(6770087828699273648)
XLA Ops:
  0.6 2.0 %shard_map.111 = (bf16[512,256]{1,0:T(8,128)(2,1)}, bf16[2,512,256]{2,1,0:T(8,128)(2,1)}) custom-call(s32[16,32]{1,0:T(8,128)} %bitcast.34, s32[1,32]{1,0:T(1,128)} %counts_ref.1, bf16[256,128]{1,0:T(8,128)(2,1)} %tokens_ref.1, bf16[256,128]{1,0:T(8,128)(2,1)} %cotangent_ref.1), custom_call_target="tpu_custom_call" | custom-call | tf_op jit(solution)/shard_map/pallas_call | solution.py:274
  2.6 14.8 %all-to-all-start = ((bf16[64,16,256]{2,1,0:T(8,128)(2,1)}), bf16[64,16,256]{2,1,0:T(8,128)(2,1)S(1)}, u32[]{:S(2)}, u32[]{:S(2)}) async-start(bf16[64,16,256]{2,1,0:T(8,128)(2,1)} %bitcast.33), calls=%async_computation | async-start | bytes 1048576 | tf_op jit(solution)/shard_map/all_to_all | solution.py:281
  17.5 0.1 pad_add_fusion.order_ref
  17.6 0.1 pad_add_fusion.1.order_ref
  17.7 17.1 %all-to-all-done = bf16[64,16,256]{2,1,0:T(8,128)(2,1)S(1)} async-done(((bf16[64,16,256]{2,1,0:T(8,128)(2,1)}), bf16[64,16,256]{2,1,0:T(8,128)(2,1)S(1)}, u32[]{:S(2)}, u32[]{:S(2)}) %all-to-all-start) | async-done | bytes 524320 | tf_op jit(solution)/shard_map/all_to_all | solution.py:281
  34.8 0.1 shard_map.112.refs_0_
  34.9 0.0 copy-start.8
  34.9 0.0 copy-start.1
  34.9 3.3 %collective-permute-start.3 = (bf16[3,512,128]{2,1,0:T(8,128)(2,1)S(1)}, bf16[3,512,128]{2,1,0:T(8,128)(2,1)S(1)}, u32[]{:S(2)}, u32[]{:S(2)}) collective-permute-start(bf16[3,512,128]{2,1,0:T(8,128)(2,1)S(1)} %shard_map.112.refs_0_), channel_id=1, source_target_pairs={{0,1},{1,2},{2,3},{3,4},{4,5},{5,6},{6,7},{7,0},{8,9},{9,10},{10,1... | collective-permute-start | bytes 1179656 | tf_op jit(solution)/shard_map/ppermute | solution.py:262
  38.2 3.8 %collective-permute-start = (bf16[3,512,128]{2,1,0:T(8,128)(2,1)S(1)}, bf16[3,512,128]{2,1,0:T(8,128)(2,1)S(1)}, u32[]{:S(2)}, u32[]{:S(2)}) collective-permute-start(bf16[3,512,128]{2,1,0:T(8,128)(2,1)S(1)} %shard_map.112.refs_0_), channel_id=1, source_target_pairs={{0,7},{1,0},{2,1},{3,2},{4,3},{5,4},{6,5},{7,6},{8,15},{9,8},{10,9... | collective-permute-start | bytes 1179656 | tf_op jit(solution)/shard_map/ppermute | solution.py:265
  42.1 7.3 %collective-permute-done.3.refs_2_ = bf16[3,512,128]{2,1,0:T(8,128)(2,1)S(1)} collective-permute-done((bf16[3,512,128]{2,1,0:T(8,128)(2,1)S(1)}, bf16[3,512,128]{2,1,0:T(8,128)(2,1)S(1)}, u32[]{:S(2)}, u32[]{:S(2)}) %collective-permute-start.3) | collective-permute-done | bytes 393248 | tf_op jit(solution)/shard_map/ppermute | solution.py:262
  49.4 1.9 %collective-permute-start.4 = (bf16[3,512,128]{2,1,0:T(8,128)(2,1)S(1)}, bf16[3,512,128]{2,1,0:T(8,128)(2,1)S(1)}, u32[]{:S(2)}, u32[]{:S(2)}) collective-permute-start(bf16[3,512,128]{2,1,0:T(8,128)(2,1)S(1)} %collective-permute-done.3.refs_2_), channel_id=1, source_target_pairs={{0,1},{1,2},{2,3},{3,4},{4,5},{5,6},{6,7},{7,0},{8,9},{9,10},{10,1... | collective-permute-start | bytes 1179656 | tf_op jit(solution)/shard_map/ppermute | solution.py:262
  51.3 0.0 collective-permute-done.refs_1_
  51.3 0.0 copy-start.4
  51.3 4.6 %collective-permute-start.1 = (bf16[3,512,128]{2,1,0:T(8,128)(2,1)S(1)}, bf16[3,512,128]{2,1,0:T(8,128)(2,1)S(1)}, u32[]{:S(2)}, u32[]{:S(2)}) collective-permute-start(bf16[3,512,128]{2,1,0:T(8,128)(2,1)S(1)} %collective-permute-done.refs_1_), channel_id=1, source_target_pairs={{0,7},{1,0},{2,1},{3,2},{4,3},{5,4},{6,5},{7,6},{8,15},{9,8},{10,9... | collective-permute-start | bytes 1179656 | tf_op jit(solution)/shard_map/ppermute | solution.py:265
  55.9 0.8 shard_map.115.own_ref
  56.7 5.1 %collective-permute-start.6 = (bf16[3,512,128]{2,1,0:T(8,128)(2,1)}, bf16[3,512,128]{2,1,0:T(8,128)(2,1)}, u32[]{:S(2)}, u32[]{:S(2)}) collective-permute-start(bf16[3,512,128]{2,1,0:T(8,128)(2,1)} %shard_map.115.own_ref), channel_id=1, source_target_pairs={{0,8},{8,0},{1,9},{9,1},{2,10},{10,2},{3,11},{11,3},{4,12},{12,4},... | collective-permute-start | bytes 1179656 | tf_op jit(solution)/shard_map/ppermute | solution.py:309
  61.8 0.5 collective-permute-done.4.refs_4_.refs_1_
  62.3 1.9 %collective-permute-start.5 = (bf16[3,512,128]{2,1,0:T(8,128)(2,1)S(1)}, bf16[3,512,128]{2,1,0:T(8,128)(2,1)S(1)}, u32[]{:S(2)}, u32[]{:S(2)}) collective-permute-start(bf16[3,512,128]{2,1,0:T(8,128)(2,1)S(1)} %collective-permute-done.4.refs_4_.refs_1_), channel_id=1, source_target_pairs={{0,1},{1,2},{2,3},{3,4},{4,5},{5,6},{6,7},{7,0},{8,9},{9,10},{10,1... | collective-permute-start | bytes 1179656 | tf_op jit(solution)/shard_map/ppermute | solution.py:262
  64.2 0.0 collective-permute-done.1.refs_3_.refs_0_
  64.2 4.6 %collective-permute-start.2 = (bf16[3,512,128]{2,1,0:T(8,128)(2,1)S(1)}, bf16[3,512,128]{2,1,0:T(8,128)(2,1)S(1)}, u32[]{:S(2)}, u32[]{:S(2)}) collective-permute-start(bf16[3,512,128]{2,1,0:T(8,128)(2,1)S(1)} %collective-permute-done.1.refs_3_.refs_0_), channel_id=1, source_target_pairs={{0,7},{1,0},{2,1},{3,2},{4,3},{5,4},{6,5},{7,6},{8,15},{9,8},{10,9... | collective-permute-start | bytes 1179656 | tf_op jit(solution)/shard_map/ppermute | solution.py:265
  68.8 0.1 copy.14.refs_6_.refs_7_.refs_5_
  68.9 0.0 copy-start.3
  69.0 1.0 copy-done.3
  69.9 1.0 copy-done.5
  70.9 2.0 %shard_map.113.refs_5_ = f32[512,256]{1,0:T(8,128)S(1)} custom-call(s32[16]{0:T(128)S(1)} %pad_add_fusion.order_ref, bf16[3,512,128]{2,1,0:T(8,128)(2,1)S(1)} %shard_map.112.refs_0_, bf16[3,512,128]{2,1,0:T(8,128)(2,1)S(1)} %copy-done.5, bf16[3,512,128]{2,1,0:T(8,128)(2,1)S(1)} %copy-done.3, bf16[3,512,128]{2,1,0:T(8,128)(2,1)S(1)} %collective-permute-done.1.refs_3_.refs_0_, ...), custom_call_target="tpu_custom_call" | custom-call | flops 335544320 | bytes 4194304 | tf_op jit(solution)/shard_map/pallas_call | solution.py:326
  73.0 2.0 %shard_map.114.refs_6_ = bf16[256,2048]{1,0:T(8,128)(2,1)} custom-call(s32[16]{0:T(128)S(1)} %pad_add_fusion.order_ref, bf16[3,512,128]{2,1,0:T(8,128)(2,1)S(1)} %shard_map.112.refs_0_, bf16[3,512,128]{2,1,0:T(8,128)(2,1)S(1)} %copy-done.5, bf16[3,512,128]{2,1,0:T(8,128)(2,1)S(1)} %copy-done.3, ...), custom_call_target="tpu_custom_call" | custom-call | flops 335544320 | bytes 4194304 | tf_op jit(solution)/shard_map/pallas_call | solution.py:335
  75.0 0.0 collective-permute-done.5.refs_0_.refs_3_
  75.1 0.1 collective-permute-done.2.refs_1_.refs_2_
  75.2 3.0 %collective-permute-start.7 = (bf16[2,512,128]{2,1,0:T(8,128)(2,1)S(1)}, bf16[2,512,128]{2,1,0:T(8,128)(2,1)S(1)}, u32[]{:S(2)}, u32[]{:S(2)}) collective-permute-start(bf16[2,512,128]{2,1,0:T(8,128)(2,1)S(1)} %slice.6), channel_id=1, source_target_pairs={{0,1},{1,2},{2,3},{3,4},{4,5},{5,6},{6,7},{7,0},{8,9},{9,10},{10,1... | collective-permute-start | bytes 786440 | tf_op jit(solution)/shard_map/ppermute | solution.py:262
  78.2 0.0 copy-start
  78.2 4.4 %collective-permute-start.8 = (bf16[1,512,128]{2,1,0:T(8,128)(2,1)S(1)}, bf16[1,512,128]{2,1,0:T(8,128)(2,1)S(1)}, u32[]{:S(2)}, u32[]{:S(2)}) collective-permute-start(bf16[1,512,128]{2,1,0:T(8,128)(2,1)S(1)} %slice.7), channel_id=1, source_target_pairs={{0,7},{1,0},{2,1},{3,2},{4,3},{5,4},{6,5},{7,6},{8,15},{9,8},{10,9... | collective-permute-start | bytes 393224 | tf_op jit(solution)/shard_map/ppermute | solution.py:265
  82.6 2.4 %collective-permute-done.8.refs_3_ = bf16[1,512,128]{2,1,0:T(8,128)(2,1)S(1)} collective-permute-done((bf16[1,512,128]{2,1,0:T(8,128)(2,1)S(1)}, bf16[1,512,128]{2,1,0:T(8,128)(2,1)S(1)}, u32[]{:S(2)}, u32[]{:S(2)}) %collective-permute-start.8) | collective-permute-done | bytes 131104 | tf_op jit(solution)/shard_map/ppermute | solution.py:265
  85.0 0.0 collective-permute-done.7.refs_2_.refs_4_
  85.0 2.1 %shard_map.116 = (bf16[512,256]{1,0:T(8,128)(2,1)S(1)}, f32[16,128]{1,0:T(8,128)S(1)}) custom-call(s32[16]{0:T(128)S(1)} %pad_add_fusion.order_ref, bf16[3,512,128]{2,1,0:T(8,128)(2,1)S(1)} %collective-permute-done.5.refs_0_.refs_3_, bf16[3,512,128]{2,1,0:T(8,128)(2,1)S(1)} %collective-permute-done.2.refs_1_.refs_2_, ...), custom_call_target="tpu_custom_call" | custom-call | flops 201326592 | bytes 3145728 | tf_op jit(solution)/shard_map/pallas_call | solution.py:352
  87.2 0.9 shard_map.117
  88.0 4.0 %collective-permute-start.9 = (bf16[1,528,128]{2,1,0:T(8,128)(2,1)S(1)}, bf16[1,528,128]{2,1,0:T(8,128)(2,1)S(1)}, u32[]{:S(2)}, u32[]{:S(2)}) collective-permute-start(bf16[1,528,128]{2,1,0:T(8,128)(2,1)S(1)} %shard_map.117), channel_id=1, source_target_pairs={{0,1},{1,2},{2,3},{3,4},{4,5},{5,6},{6,7},{7,0},{8,9},{9,10},{10,1... | collective-permute-start | bytes 405512 | tf_op jit(solution)/shard_map/ppermute | solution.py:262
  92.1 0.9 shard_map.124
  92.9 2.5 %collective-permute-start.14 = (bf16[1,528,128]{2,1,0:T(8,128)(2,1)S(1)}, bf16[1,528,128]{2,1,0:T(8,128)(2,1)S(1)}, u32[]{:S(2)}, u32[]{:S(2)}) collective-permute-start(bf16[1,528,128]{2,1,0:T(8,128)(2,1)S(1)} %shard_map.124), channel_id=1, source_target_pairs={{0,7},{1,0},{2,1},{3,2},{4,3},{5,4},{6,5},{7,6},{8,15},{9,8},{10,9... | collective-permute-start | bytes 405512 | tf_op jit(solution)/shard_map/ppermute | solution.py:265
  95.4 1.0 shard_map.118
  96.5 3.1 %collective-permute-start.10 = (bf16[2,528,128]{2,1,0:T(8,128)(2,1)S(1)}, bf16[2,528,128]{2,1,0:T(8,128)(2,1)S(1)}, u32[]{:S(2)}, u32[]{:S(2)}) collective-permute-start(bf16[2,528,128]{2,1,0:T(8,128)(2,1)S(1)} %get-tuple-element.46), channel_id=1, source_target_pairs={{0,1},{1,2},{2,3},{3,4},{4,5},{5,6},{6,7},{7,0},{8,9},{9,10},{10,1... | collective-permute-start | bytes 811016 | tf_op jit(solution)/shard_map/ppermute | solution.py:262
  99.5 0.0 collective-permute-done.14.came
  99.6 1.0 shard_map.125
  100.6 3.4 %collective-permute-start.15 = (bf16[2,528,128]{2,1,0:T(8,128)(2,1)S(1)}, bf16[2,528,128]{2,1,0:T(8,128)(2,1)S(1)}, u32[]{:S(2)}, u32[]{:S(2)}) collective-permute-start(bf16[2,528,128]{2,1,0:T(8,128)(2,1)S(1)} %get-tuple-element.56), channel_id=1, source_target_pairs={{0,7},{1,0},{2,1},{3,2},{4,3},{5,4},{6,5},{7,6},{8,15},{9,8},{10,9... | collective-permute-start | bytes 811016 | tf_op jit(solution)/shard_map/ppermute | solution.py:265
  104.1 6.3 %collective-permute-start.13 = (bf16[5,512,128]{2,1,0:T(8,128)(2,1)S(1)}, bf16[5,512,128]{2,1,0:T(8,128)(2,1)S(1)}, u32[]{:S(2)}, u32[]{:S(2)}) collective-permute-start(bf16[5,512,128]{2,1,0:T(8,128)(2,1)S(1)} %shard_map.123.own_ref), channel_id=1, source_target_pairs={{0,8},{8,0},{1,9},{9,1},{2,10},{10,2},{3,11},{11,3},{4,12},{12,4},... | collective-permute-start | bytes 1966088 | tf_op jit(solution)/shard_map/ppermute | solution.py:309
  110.4 1.0 shard_map.119
  111.4 1.9 %collective-permute-start.11 = (bf16[2,528,128]{2,1,0:T(8,128)(2,1)S(1)}, bf16[2,528,128]{2,1,0:T(8,128)(2,1)S(1)}, u32[]{:S(2)}, u32[]{:S(2)}) collective-permute-start(bf16[2,528,128]{2,1,0:T(8,128)(2,1)S(1)} %get-tuple-element.48), channel_id=1, source_target_pairs={{0,1},{1,2},{2,3},{3,4},{4,5},{5,6},{6,7},{7,0},{8,9},{9,10},{10,1... | collective-permute-start | bytes 811016 | tf_op jit(solution)/shard_map/ppermute | solution.py:262
  113.3 1.0 shard_map.126
  114.3 4.6 %collective-permute-start.16 = (bf16[2,528,128]{2,1,0:T(8,128)(2,1)S(1)}, bf16[2,528,128]{2,1,0:T(8,128)(2,1)S(1)}, u32[]{:S(2)}, u32[]{:S(2)}) collective-permute-start(bf16[2,528,128]{2,1,0:T(8,128)(2,1)S(1)} %get-tuple-element.58), channel_id=1, source_target_pairs={{0,7},{1,0},{2,1},{3,2},{4,3},{5,4},{6,5},{7,6},{8,15},{9,8},{10,9... | collective-permute-start | bytes 811016 | tf_op jit(solution)/shard_map/ppermute | solution.py:265
  118.9 1.9 %shard_map.120 = bf16[256,2048]{1,0:T(8,128)(2,1)} custom-call(s32[16]{0:T(128)S(1)} %pad_add_fusion.order_ref, bf16[3,512,128]{2,1,0:T(8,128)(2,1)S(1)} %collective-permute-done.5.refs_0_.refs_3_, bf16[3,512,128]{2,1,0:T(8,128)(2,1)S(1)} %collective-permute-done.2.refs_1_.refs_2_, ...), custom_call_target="tpu_custom_call", output_to_operand_aliasing={{}: (7, {})} | custom-call | flops 201326592 | bytes 3145728 | tf_op jit(solution)/shard_map/pallas_call | solution.py:362
  120.8 0.0 collective-permute-done.11.came
  120.8 1.0 shard_map.121
  121.8 1.9 %collective-permute-start.12 = (bf16[2,528,128]{2,1,0:T(8,128)(2,1)S(1)}, bf16[2,528,128]{2,1,0:T(8,128)(2,1)S(1)}, u32[]{:S(2)}, u32[]{:S(2)}) collective-permute-start(bf16[2,528,128]{2,1,0:T(8,128)(2,1)S(1)} %get-tuple-element.52), channel_id=1, source_target_pairs={{0,1},{1,2},{2,3},{3,4},{4,5},{5,6},{6,7},{7,0},{8,9},{9,10},{10,1... | collective-permute-start | bytes 811016 | tf_op jit(solution)/shard_map/ppermute | solution.py:262
  123.7 1.0 shard_map.127
  124.7 4.6 %collective-permute-start.17 = (bf16[2,528,128]{2,1,0:T(8,128)(2,1)S(1)}, bf16[2,528,128]{2,1,0:T(8,128)(2,1)S(1)}, u32[]{:S(2)}, u32[]{:S(2)}) collective-permute-start(bf16[2,528,128]{2,1,0:T(8,128)(2,1)S(1)} %get-tuple-element.60), channel_id=1, source_target_pairs={{0,7},{1,0},{2,1},{3,2},{4,3},{5,4},{6,5},{7,6},{8,15},{9,8},{10,9... | collective-permute-start | bytes 811016 | tf_op jit(solution)/shard_map/ppermute | solution.py:265
  129.3 2.3 %shard_map.122.refs_0_ = bf16[2048,256]{1,0:T(8,128)(2,1)} custom-call(s32[16]{0:T(128)S(1)} %pad_add_fusion.1.order_ref, bf16[3,512,128]{2,1,0:T(8,128)(2,1)} %shard_map.115.own_ref, bf16[3,512,128]{2,1,0:T(8,128)(2,1)} %collective-permute-done.6.other_ref, bf16[512,256]{1,0:T(8,128)(2,1)S(1)} %get-tuple-element.44.pre_grad_ref), custom_call_target="tpu_custom_call" | custom-call | flops 268435456 | bytes 4194304 | tf_op jit(solution)/shard_map/pallas_call | solution.py:411
  131.6 1.1 collective-permute-done.17.from_right
  132.7 1.7 %shard_map.128 = (bf16[2,512,128]{2,1,0:T(8,128)(2,1)}, f32[4,128]{1,0:T(4,128)S(1)}) custom-call(s32[16]{0:T(128)S(1)} %pad_add_fusion.order_ref, bf16[2,528,128]{2,1,0:T(8,128)(2,1)S(1)} %collective-permute-done.12.from_left, bf16[2,528,128]{2,1,0:T(8,128)(2,1)S(1)} %collective-permute-done.17.from_right, ...), custom_call_target="tpu_custom_call" | custom-call | flops 67108864 | bytes 2097152 | tf_op jit(solution)/shard_map/pallas_call | solution.py:426
  134.4 11.7 %all-to-all-start.1 = ((bf16[64,16,128]{2,1,0:T(8,128)(2,1)}), bf16[64,16,128]{2,1,0:T(8,128)(2,1)S(1)}, u32[]{:S(2)}, u32[]{:S(2)}) async-start(bf16[64,16,128]{2,1,0:T(8,128)(2,1)} %bitcast.9), calls=%async_computation.1 | async-start | bytes 524288 | tf_op jit(solution)/shard_map/all_to_all | solution.py:436
  146.1 5.0 %collective-permute-start.18 = (f32[4,128]{1,0:T(4,128)S(1)}, f32[4,128]{1,0:T(4,128)S(1)}, u32[]{:S(2)}, u32[]{:S(2)}) collective-permute-start(f32[4,128]{1,0:T(4,128)S(1)} %get-tuple-element.67), channel_id=1, source_target_pairs={{0,8},{8,0},{1,9},{9,1},{2,10},{10,2},{3,11},{11,3},{4,12},{12,4},... | collective-permute-start | bytes 6152 | tf_op jit(solution)/shard_map/ppermute | solution.py:435
  151.2 1.9 %shard_map.130 = bf16[2048,256]{1,0:T(8,128)(2,1)} custom-call(s32[16]{0:T(128)S(1)} %pad_add_fusion.1.order_ref, bf16[5,512,128]{2,1,0:T(8,128)(2,1)S(1)} %shard_map.123.own_ref, bf16[5,512,128]{2,1,0:T(8,128)(2,1)S(1)} %collective-permute-done.13.other_ref, bf16[512,256]{1,0:T(8,128)(2,1)S(1)} %get-tuple-element.44.pre_grad_ref, ...), custom_call_target="tpu_custom_call", output_to_operand_aliasing={{}: (4, {})} | custom-call | flops 268435456 | bytes 4194304 | tf_op jit(solution)/shard_map/pallas_call | solution.py:419
  153.0 0.6 add.38
  153.6 4.5 %all-to-all-done.1 = bf16[64,16,128]{2,1,0:T(8,128)(2,1)S(1)} async-done(((bf16[64,16,128]{2,1,0:T(8,128)(2,1)}), bf16[64,16,128]{2,1,0:T(8,128)(2,1)S(1)}, u32[]{:S(2)}, u32[]{:S(2)}) %all-to-all-start.1) | async-done | bytes 262176 | tf_op jit(solution)/shard_map/all_to_all | solution.py:436
  158.1 0.9 shard_map.129
  (25 shorter events, 0.1 us)
Async XLA Ops:
  2.6 32.2 %all-to-all-start = ((bf16[64,16,256]{2,1,0:T(8,128)(2,1)}), bf16[64,16,256]{2,1,0:T(8,128)(2,1)S(1)}, u32[]{:S(2)}, u32[]{:S(2)}) async-start(bf16[64,16,256]{2,1,0:T(8,128)(2,1)} %bitcast.33), calls=%async_computation | async-start | bytes 1048576 | tf_op jit(solution)/shard_map/all_to_all | solution.py:281
  34.9 33.9 %copy-start.8 = (f32[1,512]{1,0:T(1,128)S(1)}, f32[1,512]{1,0:T(1,128)}, u32[]{:S(2)}) copy-start(f32[1,512]{1,0:T(1,128)} %param.13) | copy-start | bytes 6148
  34.9 34.0 %copy-start.1 = (bf16[1,256,2048]{2,1,0:T(8,128)(2,1)S(1)}, bf16[1,256,2048]{2,1,0:T(8,128)(2,1)}, u32[]{:S(2)}) copy-start(bf16[1,256,2048]{2,1,0:T(8,128)(2,1)} %param.11) | copy-start | bytes 3145732
  34.9 14.5 %collective-permute-start.3 = (bf16[3,512,128]{2,1,0:T(8,128)(2,1)S(1)}, bf16[3,512,128]{2,1,0:T(8,128)(2,1)S(1)}, u32[]{:S(2)}, u32[]{:S(2)}) collective-permute-start(bf16[3,512,128]{2,1,0:T(8,128)(2,1)S(1)} %shard_map.112.refs_0_), channel_id=1, source_target_pairs={{0,1},{1,2},{2,3},{3,4},{4,5},{5,6},{6,7},{7,0},{8,9},{9,10},{10,1... | collective-permute-start | bytes 1179656 | tf_op jit(solution)/shard_map/ppermute | solution.py:262
  38.2 13.0 %collective-permute-start = (bf16[3,512,128]{2,1,0:T(8,128)(2,1)S(1)}, bf16[3,512,128]{2,1,0:T(8,128)(2,1)S(1)}, u32[]{:S(2)}, u32[]{:S(2)}) collective-permute-start(bf16[3,512,128]{2,1,0:T(8,128)(2,1)S(1)} %shard_map.112.refs_0_), channel_id=1, source_target_pairs={{0,7},{1,0},{2,1},{3,2},{4,3},{5,4},{6,5},{7,6},{8,15},{9,8},{10,9... | collective-permute-start | bytes 1179656 | tf_op jit(solution)/shard_map/ppermute | solution.py:265
  49.4 7.3 %copy-start.2 = (bf16[3,512,128]{2,1,0:T(8,128)(2,1)}, bf16[3,512,128]{2,1,0:T(8,128)(2,1)S(1)}, u32[]{:S(2)}) copy-start(bf16[3,512,128]{2,1,0:T(8,128)(2,1)S(1)} %collective-permute-done.3.refs_2_) | copy-start | bytes 1179652
  49.4 12.9 %collective-permute-start.4 = (bf16[3,512,128]{2,1,0:T(8,128)(2,1)S(1)}, bf16[3,512,128]{2,1,0:T(8,128)(2,1)S(1)}, u32[]{:S(2)}, u32[]{:S(2)}) collective-permute-start(bf16[3,512,128]{2,1,0:T(8,128)(2,1)S(1)} %collective-permute-done.3.refs_2_), channel_id=1, source_target_pairs={{0,1},{1,2},{2,3},{3,4},{4,5},{5,6},{6,7},{7,0},{8,9},{9,10},{10,1... | collective-permute-start | bytes 1179656 | tf_op jit(solution)/shard_map/ppermute | solution.py:262
  51.3 5.4 %copy-start.4 = (bf16[3,512,128]{2,1,0:T(8,128)(2,1)}, bf16[3,512,128]{2,1,0:T(8,128)(2,1)S(1)}, u32[]{:S(2)}) copy-start(bf16[3,512,128]{2,1,0:T(8,128)(2,1)S(1)} %collective-permute-done.refs_1_) | copy-start | bytes 1179652
  51.3 12.9 %collective-permute-start.1 = (bf16[3,512,128]{2,1,0:T(8,128)(2,1)S(1)}, bf16[3,512,128]{2,1,0:T(8,128)(2,1)S(1)}, u32[]{:S(2)}, u32[]{:S(2)}) collective-permute-start(bf16[3,512,128]{2,1,0:T(8,128)(2,1)S(1)} %collective-permute-done.refs_1_), channel_id=1, source_target_pairs={{0,7},{1,0},{2,1},{3,2},{4,3},{5,4},{6,5},{7,6},{8,15},{9,8},{10,9... | collective-permute-start | bytes 1179656 | tf_op jit(solution)/shard_map/ppermute | solution.py:265
  56.7 18.4 %collective-permute-start.6 = (bf16[3,512,128]{2,1,0:T(8,128)(2,1)}, bf16[3,512,128]{2,1,0:T(8,128)(2,1)}, u32[]{:S(2)}, u32[]{:S(2)}) collective-permute-start(bf16[3,512,128]{2,1,0:T(8,128)(2,1)} %shard_map.115.own_ref), channel_id=1, source_target_pairs={{0,8},{8,0},{1,9},{9,1},{2,10},{10,2},{3,11},{11,3},{4,12},{12,4},... | collective-permute-start | bytes 1179656 | tf_op jit(solution)/shard_map/ppermute | solution.py:309
  62.3 12.8 %collective-permute-start.5 = (bf16[3,512,128]{2,1,0:T(8,128)(2,1)S(1)}, bf16[3,512,128]{2,1,0:T(8,128)(2,1)S(1)}, u32[]{:S(2)}, u32[]{:S(2)}) collective-permute-start(bf16[3,512,128]{2,1,0:T(8,128)(2,1)S(1)} %collective-permute-done.4.refs_4_.refs_1_), channel_id=1, source_target_pairs={{0,1},{1,2},{2,3},{3,4},{4,5},{5,6},{6,7},{7,0},{8,9},{9,10},{10,1... | collective-permute-start | bytes 1179656 | tf_op jit(solution)/shard_map/ppermute | solution.py:262
  64.2 11.0 %collective-permute-start.2 = (bf16[3,512,128]{2,1,0:T(8,128)(2,1)S(1)}, bf16[3,512,128]{2,1,0:T(8,128)(2,1)S(1)}, u32[]{:S(2)}, u32[]{:S(2)}) collective-permute-start(bf16[3,512,128]{2,1,0:T(8,128)(2,1)S(1)} %collective-permute-done.1.refs_3_.refs_0_), channel_id=1, source_target_pairs={{0,7},{1,0},{2,1},{3,2},{4,3},{5,4},{6,5},{7,6},{8,15},{9,8},{10,9... | collective-permute-start | bytes 1179656 | tf_op jit(solution)/shard_map/ppermute | solution.py:265
  68.9 1.0 copy-start.3
  69.9 1.0 copy-start.5
  70.9 2.1 %copy-start.6 = (bf16[1,512,256]{2,1,0:T(8,128)(2,1)S(1)}, bf16[1,512,256]{2,1,0:T(8,128)(2,1)}, u32[]{:S(2)}) copy-start(bf16[1,512,256]{2,1,0:T(8,128)(2,1)} %param.12) | copy-start | bytes 786436
  75.2 9.8 %collective-permute-start.7 = (bf16[2,512,128]{2,1,0:T(8,128)(2,1)S(1)}, bf16[2,512,128]{2,1,0:T(8,128)(2,1)S(1)}, u32[]{:S(2)}, u32[]{:S(2)}) collective-permute-start(bf16[2,512,128]{2,1,0:T(8,128)(2,1)S(1)} %slice.6), channel_id=1, source_target_pairs={{0,1},{1,2},{2,3},{3,4},{4,5},{5,6},{6,7},{7,0},{8,9},{9,10},{10,1... | collective-permute-start | bytes 786440 | tf_op jit(solution)/shard_map/ppermute | solution.py:262
  78.2 9.0 %copy-start = (bf16[1,2048,256]{2,1,0:T(8,128)(2,1)S(1)}, bf16[1,2048,256]{2,1,0:T(8,128)(2,1)}, u32[]{:S(2)}) copy-start(bf16[1,2048,256]{2,1,0:T(8,128)(2,1)} %param.10) | copy-start | bytes 3145732
  78.2 6.8 %collective-permute-start.8 = (bf16[1,512,128]{2,1,0:T(8,128)(2,1)S(1)}, bf16[1,512,128]{2,1,0:T(8,128)(2,1)S(1)}, u32[]{:S(2)}, u32[]{:S(2)}) collective-permute-start(bf16[1,512,128]{2,1,0:T(8,128)(2,1)S(1)} %slice.7), channel_id=1, source_target_pairs={{0,7},{1,0},{2,1},{3,2},{4,3},{5,4},{6,5},{7,6},{8,15},{9,8},{10,9... | collective-permute-start | bytes 393224 | tf_op jit(solution)/shard_map/ppermute | solution.py:265
  88.0 7.4 %collective-permute-start.9 = (bf16[1,528,128]{2,1,0:T(8,128)(2,1)S(1)}, bf16[1,528,128]{2,1,0:T(8,128)(2,1)S(1)}, u32[]{:S(2)}, u32[]{:S(2)}) collective-permute-start(bf16[1,528,128]{2,1,0:T(8,128)(2,1)S(1)} %shard_map.117), channel_id=1, source_target_pairs={{0,1},{1,2},{2,3},{3,4},{4,5},{5,6},{6,7},{7,0},{8,9},{9,10},{10,1... | collective-permute-start | bytes 405512 | tf_op jit(solution)/shard_map/ppermute | solution.py:262
  92.9 6.6 %collective-permute-start.14 = (bf16[1,528,128]{2,1,0:T(8,128)(2,1)S(1)}, bf16[1,528,128]{2,1,0:T(8,128)(2,1)S(1)}, u32[]{:S(2)}, u32[]{:S(2)}) collective-permute-start(bf16[1,528,128]{2,1,0:T(8,128)(2,1)S(1)} %shard_map.124), channel_id=1, source_target_pairs={{0,7},{1,0},{2,1},{3,2},{4,3},{5,4},{6,5},{7,6},{8,15},{9,8},{10,9... | collective-permute-start | bytes 405512 | tf_op jit(solution)/shard_map/ppermute | solution.py:265
  96.5 13.9 %collective-permute-start.10 = (bf16[2,528,128]{2,1,0:T(8,128)(2,1)S(1)}, bf16[2,528,128]{2,1,0:T(8,128)(2,1)S(1)}, u32[]{:S(2)}, u32[]{:S(2)}) collective-permute-start(bf16[2,528,128]{2,1,0:T(8,128)(2,1)S(1)} %get-tuple-element.46), channel_id=1, source_target_pairs={{0,1},{1,2},{2,3},{3,4},{4,5},{5,6},{6,7},{7,0},{8,9},{9,10},{10,1... | collective-permute-start | bytes 811016 | tf_op jit(solution)/shard_map/ppermute | solution.py:262
  100.6 12.7 %collective-permute-start.15 = (bf16[2,528,128]{2,1,0:T(8,128)(2,1)S(1)}, bf16[2,528,128]{2,1,0:T(8,128)(2,1)S(1)}, u32[]{:S(2)}, u32[]{:S(2)}) collective-permute-start(bf16[2,528,128]{2,1,0:T(8,128)(2,1)S(1)} %get-tuple-element.56), channel_id=1, source_target_pairs={{0,7},{1,0},{2,1},{3,2},{4,3},{5,4},{6,5},{7,6},{8,15},{9,8},{10,9... | collective-permute-start | bytes 811016 | tf_op jit(solution)/shard_map/ppermute | solution.py:265
  104.1 27.5 %collective-permute-start.13 = (bf16[5,512,128]{2,1,0:T(8,128)(2,1)S(1)}, bf16[5,512,128]{2,1,0:T(8,128)(2,1)S(1)}, u32[]{:S(2)}, u32[]{:S(2)}) collective-permute-start(bf16[5,512,128]{2,1,0:T(8,128)(2,1)S(1)} %shard_map.123.own_ref), channel_id=1, source_target_pairs={{0,8},{8,0},{1,9},{9,1},{2,10},{10,2},{3,11},{11,3},{4,12},{12,4},... | collective-permute-start | bytes 1966088 | tf_op jit(solution)/shard_map/ppermute | solution.py:309
  111.4 9.4 %collective-permute-start.11 = (bf16[2,528,128]{2,1,0:T(8,128)(2,1)S(1)}, bf16[2,528,128]{2,1,0:T(8,128)(2,1)S(1)}, u32[]{:S(2)}, u32[]{:S(2)}) collective-permute-start(bf16[2,528,128]{2,1,0:T(8,128)(2,1)S(1)} %get-tuple-element.48), channel_id=1, source_target_pairs={{0,1},{1,2},{2,3},{3,4},{4,5},{5,6},{6,7},{7,0},{8,9},{9,10},{10,1... | collective-permute-start | bytes 811016 | tf_op jit(solution)/shard_map/ppermute | solution.py:262
  114.3 9.4 %collective-permute-start.16 = (bf16[2,528,128]{2,1,0:T(8,128)(2,1)S(1)}, bf16[2,528,128]{2,1,0:T(8,128)(2,1)S(1)}, u32[]{:S(2)}, u32[]{:S(2)}) collective-permute-start(bf16[2,528,128]{2,1,0:T(8,128)(2,1)S(1)} %get-tuple-element.58), channel_id=1, source_target_pairs={{0,7},{1,0},{2,1},{3,2},{4,3},{5,4},{6,5},{7,6},{8,15},{9,8},{10,9... | collective-permute-start | bytes 811016 | tf_op jit(solution)/shard_map/ppermute | solution.py:265
  121.8 9.8 %collective-permute-start.12 = (bf16[2,528,128]{2,1,0:T(8,128)(2,1)S(1)}, bf16[2,528,128]{2,1,0:T(8,128)(2,1)S(1)}, u32[]{:S(2)}, u32[]{:S(2)}) collective-permute-start(bf16[2,528,128]{2,1,0:T(8,128)(2,1)S(1)} %get-tuple-element.52), channel_id=1, source_target_pairs={{0,1},{1,2},{2,3},{3,4},{4,5},{5,6},{6,7},{7,0},{8,9},{9,10},{10,1... | collective-permute-start | bytes 811016 | tf_op jit(solution)/shard_map/ppermute | solution.py:262
  124.7 8.0 %collective-permute-start.17 = (bf16[2,528,128]{2,1,0:T(8,128)(2,1)S(1)}, bf16[2,528,128]{2,1,0:T(8,128)(2,1)S(1)}, u32[]{:S(2)}, u32[]{:S(2)}) collective-permute-start(bf16[2,528,128]{2,1,0:T(8,128)(2,1)S(1)} %get-tuple-element.60), channel_id=1, source_target_pairs={{0,7},{1,0},{2,1},{3,2},{4,3},{5,4},{6,5},{7,6},{8,15},{9,8},{10,9... | collective-permute-start | bytes 811016 | tf_op jit(solution)/shard_map/ppermute | solution.py:265
  134.4 23.7 %all-to-all-start.1 = ((bf16[64,16,128]{2,1,0:T(8,128)(2,1)}), bf16[64,16,128]{2,1,0:T(8,128)(2,1)S(1)}, u32[]{:S(2)}, u32[]{:S(2)}) async-start(bf16[64,16,128]{2,1,0:T(8,128)(2,1)} %bitcast.9), calls=%async_computation.1 | async-start | bytes 524288 | tf_op jit(solution)/shard_map/all_to_all | solution.py:436
  146.1 12.0 %copy-start.7 = (bf16[512,256]{1,0:T(8,128)(2,1)S(1)}, bf16[512,256]{1,0:T(8,128)(2,1)}, u32[]{:S(2)}) copy-start(bf16[512,256]{1,0:T(8,128)(2,1)} %get-tuple-element.36.sel_ref) | copy-start | bytes 786436
  146.1 6.9 %collective-permute-start.18 = (f32[4,128]{1,0:T(4,128)S(1)}, f32[4,128]{1,0:T(4,128)S(1)}, u32[]{:S(2)}, u32[]{:S(2)}) collective-permute-start(f32[4,128]{1,0:T(4,128)S(1)} %get-tuple-element.67), channel_id=1, source_target_pairs={{0,8},{8,0},{1,9},{9,1},{2,10},{10,2},{3,11},{11,3},{4,12},{12,4},... | collective-permute-start | bytes 6152 | tf_op jit(solution)/shard_map/ppermute | solution.py:435
